TPU v7x, 128 devices: a whole 4x4x4 slice. The times are simulated.
128 devices in a mesh: rep: 2 (over z_lo), shard: 16 (over y, z_hi, core), ctx: 4 (over x).
Axes of the slice: x: 4, y: 4, z: 4 (z_hi: 2, z_lo: 2; z = z_hi * 2 + z_lo), core: 2. Of those that a mesh axis runs over, the one named last changes fastest.
Arguments:
- image_tokens: bfloat16 [32, 384, 1536], P(('rep', 'shard'), 'ctx'), may hold values from -6 to 6
- text_tokens: bfloat16 [32, 160, 1536], P(('rep', 'shard'), 'ctx'), may hold values from -6 to 6
- text_lengths: int32 [32, 4], P(('rep', 'shard'), 'ctx'), may hold values from 1 to 40, 154 in all within a row
- slot_sequence: int32 [32], P(('rep', 'shard')), may hold values from -1 to 26, as said below
- conditioning: bfloat16 [27, 1536], replicated, may hold values from -6 to 6
- mod_weight: bfloat16 [1536, 2, 9216], P(('shard', 'ctx')), may hold values from -0.15625 to 0.15625
- mod_bias: bfloat16 [2, 9216], replicated, may hold values from -3 to 3
- qkv_weight: bfloat16 [1536, 2, 4608], P(('shard', 'ctx')), may hold values from -0.15625 to 0.15625
- qv_bias: bfloat16 [2, 3072], replicated, may hold values from -2 to 2
- out_weight: bfloat16 [1536, 2, 1536], P(('shard', 'ctx')), may hold values from -0.625 to 0.625
- out_bias: bfloat16 [2, 1536], replicated, may hold values from -2 to 2
- up_weight: bfloat16 [1536, 2, 6144], P(('shard', 'ctx')), may hold values from -0.15625 to 0.15625
- up_bias: bfloat16 [2, 6144], replicated, may hold values from -2 to 2
- down_weight: bfloat16 [6144, 2, 1536], P(('shard', 'ctx')), may hold values from -0.078125 to 0.078125
- down_bias: bfloat16 [2, 1536], replicated, may hold values from -2 to 2
- image_cotan: bfloat16 [32, 384, 1536], P(('rep', 'shard'), 'ctx'), may hold values from -6 to 6
- text_cotan: bfloat16 [32, 160, 1536], P(('rep', 'shard'), 'ctx'), may hold values from -6 to 6
Outputs:
- image_out: bfloat16 [32, 384, 1536], P(('rep', 'shard'), 'ctx')
- text_out: bfloat16 [32, 160, 1536], P(('rep', 'shard'), 'ctx')
- image_grad: float32 [32, 384, 1536], P(('rep', 'shard'), 'ctx')
- text_grad: float32 [32, 160, 1536], P(('rep', 'shard'), 'ctx')
- cond_grad: float32 [27, 1536], P(None, ('shard', 'ctx'))
- mod_weight_grad: float32 [1536, 2, 9216], P(('shard', 'ctx'))
- mod_bias_grad: float32 [2, 9216], P(None, ('shard', 'ctx'))
- qkv_weight_grad: float32 [1536, 2, 4608], P(('shard', 'ctx'))
- qv_bias_grad: float32 [2, 3072], P(None, ('shard', 'ctx'))
- out_weight_grad: float32 [1536, 2, 1536], P(('shard', 'ctx'))
- out_bias_grad: float32 [2, 1536], P(None, ('shard', 'ctx'))
- up_weight_grad: float32 [1536, 2, 6144], P(('shard', 'ctx'))
- up_bias_grad: float32 [2, 6144], P(None, ('shard', 'ctx'))
- down_weight_grad: float32 [6144, 2, 1536], P(('shard', 'ctx'))
- down_bias_grad: float32 [2, 1536], P(None, ('shard', 'ctx'))
Inputs may be any that keep to these rules, and one draw needn't show every extreme that they name: `slot_sequence`: each of the 27 sequences stands in exactly one slot; the other slots hold -1. `text_lengths`: each slot's row sums to 154.
All inputs are finite; a program needn't handle non-finite values. No bound on the sum of `text_lengths` on one device may be relied on, other than what follows from the above.
Results may differ from a plain program's by a relative error of at most 0.02.
Values may be sent and summed in bfloat16 or wider, within the bound.
No kernel may reach another device: no remote copies, remote signals or barrier semaphores. Data moves between devices by JAX's collectives and lax.ppermute only.
A program may use at most 192 MiB of HBM per device.

v0:
```python
import jax
import jax.numpy as jnp
from jax import lax
from jax.sharding import PartitionSpec as P

HEAD_DIM = 64


def norm_rows(values):
    center = values - jnp.mean(values, axis=-1, keepdims=True)
    inv_scale = lax.rsqrt(jnp.mean(center * center, axis=-1, keepdims=True) + 1e-06)
    return (center * inv_scale, inv_scale)


def norm_back(grad_out, normed, inv_scale):
    return inv_scale * (
        grad_out
        - jnp.mean(grad_out, axis=-1, keepdims=True)
        - normed * jnp.mean(grad_out * normed, axis=-1, keepdims=True)
    )


def gelu_tanh(values):
    return jax.nn.gelu(values, approximate=True)


def split_heads(matrix):
    return matrix.reshape(matrix.shape[0], -1, HEAD_DIM)


def joint_scores(query, all_keys, all_bias):
    scores = jnp.einsum(
        "qhd,khd->hqk",
        split_heads(query),
        split_heads(all_keys),
        preferred_element_type=jnp.float32,
    )
    return scores * 0.125 + all_bias[None, None, :]


def attention_forward(query, all_keys, all_values, all_bias):
    scores = joint_scores(query, all_keys, all_bias)
    top_score = jnp.max(scores, axis=-1, keepdims=True)
    exp_scores = jnp.exp(scores - top_score)
    row_total = jnp.sum(exp_scores, axis=-1, keepdims=True)
    log_total = top_score + jnp.log(row_total)
    weights = (exp_scores / row_total).astype(jnp.bfloat16)
    mixed = jnp.einsum(
        "hqk,khd->qhd", weights, split_heads(all_values), preferred_element_type=jnp.float32
    )
    return (mixed.reshape(query.shape[0], query.shape[1]).astype(jnp.bfloat16), log_total)


def attention_backward(query, all_keys, all_values, all_bias, log_total, grad_mixed):
    grad_heads = split_heads(grad_mixed)
    probs = jnp.exp(joint_scores(query, all_keys, all_bias) - log_total)
    grad_probs = jnp.einsum(
        "qhd,khd->hqk", grad_heads, split_heads(all_values), preferred_element_type=jnp.float32
    )
    delta = jnp.sum(probs * grad_probs, axis=-1, keepdims=True)
    grad_scores = (probs * (grad_probs - delta)).astype(jnp.bfloat16)
    grad_query = (
        (
            jnp.einsum(
                "hqk,khd->qhd",
                grad_scores,
                split_heads(all_keys),
                preferred_element_type=jnp.float32,
            )
            * 0.125
        )
        .reshape(query.shape)
        .astype(jnp.bfloat16)
    )
    grad_keys = (
        jnp.einsum(
            "hqk,qhd->khd", grad_scores, split_heads(query), preferred_element_type=jnp.float32
        ).reshape(all_keys.shape)
        * 0.125
    )
    grad_values = jnp.einsum(
        "hqk,qhd->khd", probs.astype(jnp.bfloat16), grad_heads, preferred_element_type=jnp.float32
    ).reshape(all_keys.shape)
    return (grad_query, grad_keys, grad_values)


def first_modulated(inputs, modulation):
    saved = []
    for stream in range(2):
        shifts = modulation[stream]
        normed, inv_scale = norm_rows(inputs[stream])
        modulated = (normed * (1.0 + shifts[1]) + shifts[0]).astype(jnp.bfloat16)
        saved.append((normed, inv_scale, modulated))
    return saved


def project(modulated, qkv_cols, qv_float, stream, offset, span):
    full_width = qv_float.shape[1] // 2
    projected = jnp.dot(modulated, qkv_cols[:, stream], preferred_element_type=jnp.float32)
    query = (
        projected[:, :span] + lax.dynamic_slice_in_dim(qv_float[stream], offset, span, 0)
    ).astype(jnp.bfloat16)
    key_rows = projected[:, span : 2 * span].astype(jnp.bfloat16)
    value_rows = (
        projected[:, 2 * span :]
        + lax.dynamic_slice_in_dim(qv_float[stream], full_width + offset, span, 0)
    ).astype(jnp.bfloat16)
    return (query, key_rows, value_rows)


def stream_mod_grads(
    grad_mod_one, normed, grad_middle, attn_out, grad_mod_two, normed_two, grad_gate_two
):
    return jnp.concatenate(
        [
            jnp.sum(grad_mod_one, axis=0),
            jnp.sum(grad_mod_one * normed, axis=0),
            jnp.sum(grad_middle * attn_out, axis=0),
            jnp.sum(grad_mod_two, axis=0),
            jnp.sum(grad_mod_two * normed_two, axis=0),
            grad_gate_two,
        ]
    )


def owner_slice(values):
    width_part = values.shape[1] // lax.axis_size(("shard", "ctx"))
    return lax.dynamic_slice_in_dim(
        values, lax.axis_index(("shard", "ctx")) * width_part, width_part, 1
    )


def column_pieces(gathered, shards, splits, groups):
    row_count = gathered.shape[0] // shards
    width_part = gathered.shape[2] // (groups * splits)
    return gathered.reshape(shards, row_count, 2, groups, splits, width_part).transpose(
        4, 0, 1, 2, 3, 5
    )


def column_join(received):
    splits, shards, row_count, streams, groups, width_part = received.shape
    return received.transpose(1, 0, 2, 3, 4, 5).reshape(
        shards * splits * row_count, streams, groups * width_part
    )


def row_pieces(gathered, splits):
    return gathered.reshape((splits, gathered.shape[0] // splits) + gathered.shape[1:])


def row_join(received, shards):
    splits = received.shape[0]
    row_count = received.shape[1] * splits // shards
    shaped = received.reshape(
        splits, shards // splits, row_count, received.shape[2], received.shape[3]
    )
    return shaped.transpose(1, 0, 2, 3, 4).reshape(
        received.shape[1] * splits, received.shape[2], received.shape[3]
    )


def send_pieces(gathered_four, shards, splits):
    qkv_all, out_all, up_all, down_all = gathered_four
    return (
        column_pieces(qkv_all, shards, splits, 3),
        row_pieces(out_all, splits),
        column_pieces(up_all, shards, splits, 1),
        row_pieces(down_all, splits),
    )


def join_pieces(received_four, shards):
    qkv_got, out_got, up_got, down_got = received_four
    return (
        column_join(qkv_got),
        row_join(out_got, shards),
        column_join(up_got),
        row_join(down_got, shards),
    )


def slice_weights(qkv_weight, out_weight, up_weight, down_weight):
    shards = lax.axis_size("shard")
    splits = lax.axis_size("ctx")
    gathered = (
        lax.all_gather(qkv_weight, "shard", axis=0, tiled=True),
        lax.all_gather(out_weight, "shard", axis=0, tiled=True),
        lax.all_gather(up_weight, "shard", axis=0, tiled=True),
        lax.all_gather(down_weight, "shard", axis=0, tiled=True),
    )
    qkv_send, out_send, up_send, down_send = send_pieces(gathered, shards, splits)
    received = (
        lax.all_to_all(qkv_send, "ctx", split_axis=0, concat_axis=0, tiled=True),
        lax.all_to_all(out_send, "ctx", split_axis=0, concat_axis=0, tiled=True),
        lax.all_to_all(up_send, "ctx", split_axis=0, concat_axis=0, tiled=True),
        lax.all_to_all(down_send, "ctx", split_axis=0, concat_axis=0, tiled=True),
    )
    return join_pieces(received, shards)


def slice_weights_again(qkv_weight, out_weight, up_weight, down_weight):
    shards = lax.axis_size("shard")
    splits = lax.axis_size("ctx")
    gathered = (
        lax.all_gather(qkv_weight, "shard", axis=0, tiled=True),
        lax.all_gather(out_weight, "shard", axis=0, tiled=True),
        lax.all_gather(up_weight, "shard", axis=0, tiled=True),
        lax.all_gather(down_weight, "shard", axis=0, tiled=True),
    )
    qkv_send, out_send, up_send, down_send = send_pieces(gathered, shards, splits)
    received = (
        lax.all_to_all(qkv_send, "ctx", split_axis=0, concat_axis=0, tiled=True),
        lax.all_to_all(out_send, "ctx", split_axis=0, concat_axis=0, tiled=True),
        lax.all_to_all(up_send, "ctx", split_axis=0, concat_axis=0, tiled=True),
        lax.all_to_all(down_send, "ctx", split_axis=0, concat_axis=0, tiled=True),
    )
    return join_pieces(received, shards)


def column_grad_pieces(grad, shards, splits, groups):
    row_count = grad.shape[0] // (shards * splits)
    width_part = grad.shape[2] // groups
    return grad.reshape(shards, splits, row_count, grad.shape[1], groups, width_part).transpose(
        1, 0, 2, 3, 4, 5
    )


def column_grad_join(summed):
    splits, single, row_count, streams, groups, width_part = summed.shape
    return summed.transpose(1, 2, 3, 4, 0, 5).reshape(
        row_count, streams, groups * splits * width_part
    )


def row_grad_pieces(grad, shards, splits):
    row_count = grad.shape[0] // shards
    return grad.reshape(
        shards // splits, splits, row_count, grad.shape[1], grad.shape[2]
    ).transpose(1, 0, 2, 3, 4)


def fold_sources(received, shards):
    return jnp.sum(
        received.reshape((shards, received.shape[0] // shards) + received.shape[1:]), axis=0
    )


def to_sequence(first, second):
    return (
        lax.all_gather(first, "ctx", axis=0, tiled=True),
        lax.all_gather(second, "ctx", axis=0, tiled=True),
    )


def to_rows(first, second):
    return (
        lax.psum_scatter(first.astype(jnp.bfloat16), "ctx", scatter_dimension=0, tiled=True).astype(
            jnp.float32
        ),
        lax.psum_scatter(
            second.astype(jnp.bfloat16), "ctx", scatter_dimension=0, tiled=True
        ).astype(jnp.float32),
    )


def place_block(vector, position, splits):
    return (
        (jnp.arange(splits, dtype=jnp.int32)[:, None] == position).astype(jnp.float32)
        * vector[None, :]
    ).reshape(-1)


def heads_path(inputs, cotangents, modulation, row_masks, text_valid, weights, biases):
    qv_float, out_float, up_float, down_float = biases
    width = inputs[0].shape[1]
    splits = lax.axis_size("ctx")
    shards = lax.axis_size("shard")
    position = lax.axis_index("ctx")
    span = width // splits
    ff_span = weights[2].shape[2] // splits
    att_cols, att_rows, mlp_cols, mlp_rows = slice_weights(
        weights[0], weights[1], weights[2], weights[3]
    )
    first_saved = first_modulated(inputs, modulation)
    image_all, text_all, valid_all = (
        lax.all_gather(first_saved[0][2], "ctx", axis=0, tiled=True),
        lax.all_gather(first_saved[1][2], "ctx", axis=0, tiled=True),
        lax.all_gather(text_valid.astype(jnp.bfloat16), "ctx", axis=0, tiled=True),
    )
    image_count = image_all.shape[0]
    key_bias = jnp.concatenate(
        [
            jnp.zeros((image_count,), jnp.float32),
            (valid_all.astype(jnp.float32) - 1.0) * 1000000000.0,
        ]
    )
    seq_inputs = (image_all, text_all)
    queries, key_parts, value_parts = ([], [], [])
    for stream in range(2):
        query_part, key_part, value_part = project(
            seq_inputs[stream], att_cols, qv_float, stream, position * span, span
        )
        queries.append(query_part)
        key_parts.append(key_part)
        value_parts.append(value_part)
    query = jnp.concatenate(queries)
    all_keys = jnp.concatenate(key_parts)
    all_values = jnp.concatenate(value_parts)
    mixed, log_total = attention_forward(query, all_keys, all_values, key_bias)
    mixed_parts = (mixed[:image_count], mixed[image_count:])
    attn_image, attn_text = to_rows(
        jnp.dot(mixed_parts[0], att_rows[:, 0], preferred_element_type=jnp.float32),
        jnp.dot(mixed_parts[1], att_rows[:, 1], preferred_element_type=jnp.float32),
    )
    attn_outs = (attn_image + out_float[0], attn_text + out_float[1])
    second_saved = []
    for stream in range(2):
        shifts = modulation[stream]
        middle = inputs[stream] + shifts[2] * attn_outs[stream]
        normed_two, inv_scale_two = norm_rows(middle)
        modulated_two = (normed_two * (1.0 + shifts[4]) + shifts[3]).astype(jnp.bfloat16)
        second_saved.append((middle, normed_two, inv_scale_two, modulated_two))
    second_image, second_text = to_sequence(second_saved[0][3], second_saved[1][3])
    seq_seconds = (second_image, second_text)
    hiddens, actives, down_parts = ([], [], [])
    for stream in range(2):
        hidden = jnp.dot(
            seq_seconds[stream], mlp_cols[:, stream], preferred_element_type=jnp.float32
        ) + lax.dynamic_slice_in_dim(up_float[stream], position * ff_span, ff_span, 0)
        activated = gelu_tanh(hidden).astype(jnp.bfloat16)
        hiddens.append(hidden)
        actives.append(activated)
        down_parts.append(
            jnp.dot(activated, mlp_rows[:, stream], preferred_element_type=jnp.float32)
        )
    branch_image, branch_text = to_rows(down_parts[0], down_parts[1])
    branches = (branch_image + down_float[0], branch_text + down_float[1])
    outputs = []
    for stream in range(2):
        shifts = modulation[stream]
        outputs.append(
            ((second_saved[stream][0] + shifts[5] * branches[stream]) * row_masks[stream]).astype(
                jnp.bfloat16
            )[None]
        )
    att_cols, att_rows, mlp_cols, mlp_rows = slice_weights_again(
        weights[0], weights[1], weights[2], weights[3]
    )
    gate_grads, branch_grads = ([], [])
    for stream in range(2):
        grad_out = cotangents[stream]
        gate_grads.append(jnp.sum(grad_out * branches[stream], axis=0))
        branch_grads.append((grad_out * modulation[stream][5]).astype(jnp.bfloat16))
    branch_seq_image, branch_seq_text = to_sequence(branch_grads[0], branch_grads[1])
    seq_branch = (branch_seq_image, branch_seq_text)
    hidden_grads, second_partials = ([], [])
    for stream in range(2):
        grad_activated = jnp.einsum(
            "nd,fd->nf", seq_branch[stream], mlp_rows[:, stream], preferred_element_type=jnp.float32
        )
        grad_hidden = jax.vjp(gelu_tanh, hiddens[stream])[1](grad_activated)[0].astype(jnp.bfloat16)
        hidden_grads.append(grad_hidden)
        second_partials.append(
            jnp.einsum(
                "nf,df->nd", grad_hidden, mlp_cols[:, stream], preferred_element_type=jnp.float32
            )
        )
    grad_two_image, grad_two_text = to_rows(second_partials[0], second_partials[1])
    mod_two_grads = (grad_two_image, grad_two_text)
    middle_grads, attn_grads = ([], [])
    for stream in range(2):
        shifts = modulation[stream]
        middle, normed_two, inv_scale_two, modulated_two = second_saved[stream]
        grad_middle = cotangents[stream] + norm_back(
            mod_two_grads[stream] * (1.0 + shifts[4]), normed_two, inv_scale_two
        )
        middle_grads.append(grad_middle)
        attn_grads.append((grad_middle * shifts[2]).astype(jnp.bfloat16))
    attn_seq_image, attn_seq_text = to_sequence(attn_grads[0], attn_grads[1])
    seq_attn = (attn_seq_image, attn_seq_text)
    grad_mixed = jnp.concatenate(
        [
            jnp.einsum(
                "ne,de->nd", seq_attn[0], att_rows[:, 0], preferred_element_type=jnp.float32
            ),
            jnp.einsum(
                "ne,de->nd", seq_attn[1], att_rows[:, 1], preferred_element_type=jnp.float32
            ),
        ]
    ).astype(jnp.bfloat16)
    grad_query, grad_keys, grad_values = attention_backward(
        query, all_keys, all_values, key_bias, log_total, grad_mixed
    )
    grad_keys = grad_keys.astype(jnp.bfloat16)
    grad_values = grad_values.astype(jnp.bfloat16)
    bounds = ((0, image_count), (image_count, query.shape[0]))
    proj_grads, first_partials, qv_grads = ([], [], [])
    for stream in range(2):
        low_row, high_row = bounds[stream]
        grad_projected = jnp.concatenate(
            [
                grad_query[low_row:high_row],
                grad_keys[low_row:high_row],
                grad_values[low_row:high_row],
            ],
            axis=1,
        )
        proj_grads.append(grad_projected)
        first_partials.append(
            jnp.einsum(
                "nc,dc->nd", grad_projected, att_cols[:, stream], preferred_element_type=jnp.float32
            )
        )
        qv_grads.append(
            jnp.concatenate(
                [
                    place_block(
                        jnp.sum(grad_query[low_row:high_row].astype(jnp.float32), axis=0),
                        position,
                        splits,
                    ),
                    place_block(
                        jnp.sum(grad_values[low_row:high_row].astype(jnp.float32), axis=0),
                        position,
                        splits,
                    ),
                ]
            )
        )
    grad_one_image, grad_one_text = to_rows(first_partials[0], first_partials[1])
    mod_one_grads = (grad_one_image, grad_one_text)
    input_grads, mod_grads, out_sums, up_sums, down_sums = ([], [], [], [], [])
    for stream in range(2):
        shifts = modulation[stream]
        normed, inv_scale, modulated = first_saved[stream]
        grad_mod_one = mod_one_grads[stream]
        input_grads.append(
            (middle_grads[stream] + norm_back(grad_mod_one * (1.0 + shifts[1]), normed, inv_scale))[
                None
            ]
        )
        mod_grads.append(
            stream_mod_grads(
                grad_mod_one,
                normed,
                middle_grads[stream],
                attn_outs[stream],
                mod_two_grads[stream],
                second_saved[stream][1],
                gate_grads[stream],
            )
        )
        out_sums.append(jnp.sum(attn_grads[stream].astype(jnp.float32), axis=0))
        up_sums.append(
            place_block(jnp.sum(hidden_grads[stream].astype(jnp.float32), axis=0), position, splits)
        )
        down_sums.append(jnp.sum(branch_grads[stream].astype(jnp.float32), axis=0))
    qkv_local = jnp.stack(
        [
            jnp.einsum(
                "nr,nx->rx",
                seq_inputs[stream],
                proj_grads[stream],
                preferred_element_type=jnp.float32,
            )
            for stream in range(2)
        ],
        axis=1,
    )
    out_local = jnp.stack(
        [
            jnp.einsum(
                "nr,nx->rx",
                mixed_parts[stream],
                seq_attn[stream],
                preferred_element_type=jnp.float32,
            )
            for stream in range(2)
        ],
        axis=1,
    )
    up_local = jnp.stack(
        [
            jnp.einsum(
                "nr,nx->rx",
                seq_seconds[stream],
                hidden_grads[stream],
                preferred_element_type=jnp.float32,
            )
            for stream in range(2)
        ],
        axis=1,
    )
    down_local = jnp.stack(
        [
            jnp.einsum(
                "nr,nx->rx", actives[stream], seq_branch[stream], preferred_element_type=jnp.float32
            )
            for stream in range(2)
        ],
        axis=1,
    )
    qkv_send = column_grad_pieces(qkv_local, shards, splits, 3)
    out_send = row_grad_pieces(out_local, shards, splits)
    up_send = column_grad_pieces(up_local, shards, splits, 1)
    down_send = row_grad_pieces(down_local, shards, splits)
    qkv_got, out_got, up_got, down_got = (
        lax.all_to_all(
            qkv_send.astype(jnp.bfloat16), "ctx", split_axis=0, concat_axis=0, tiled=True
        ).astype(qkv_send.dtype),
        lax.all_to_all(
            out_send.astype(jnp.bfloat16), "ctx", split_axis=0, concat_axis=0, tiled=True
        ).astype(out_send.dtype),
        lax.all_to_all(
            up_send.astype(jnp.bfloat16), "ctx", split_axis=0, concat_axis=0, tiled=True
        ).astype(up_send.dtype),
        lax.all_to_all(
            down_send.astype(jnp.bfloat16), "ctx", split_axis=0, concat_axis=0, tiled=True
        ).astype(down_send.dtype),
    )
    out_got = out_got.reshape((1, shards) + out_got.shape[2:])
    down_got = down_got.reshape((1, shards) + down_got.shape[2:])
    qkv_recv, out_recv, up_recv, down_recv = (
        lax.all_to_all(
            qkv_got.astype(jnp.bfloat16), "shard", split_axis=1, concat_axis=0, tiled=True
        ).astype(qkv_got.dtype),
        lax.all_to_all(
            out_got.astype(jnp.bfloat16), "shard", split_axis=1, concat_axis=0, tiled=True
        ).astype(out_got.dtype),
        lax.all_to_all(
            up_got.astype(jnp.bfloat16), "shard", split_axis=1, concat_axis=0, tiled=True
        ).astype(up_got.dtype),
        lax.all_to_all(
            down_got.astype(jnp.bfloat16), "shard", split_axis=1, concat_axis=0, tiled=True
        ).astype(down_got.dtype),
    )
    qkv_sum = fold_sources(qkv_recv, shards)
    out_sum = fold_sources(out_recv, shards)
    up_sum = fold_sources(up_recv, shards)
    down_sum = fold_sources(down_recv, shards)
    grads = (
        column_grad_join(qkv_sum),
        out_sum.reshape(out_sum.shape[2:]),
        column_grad_join(up_sum),
        down_sum.reshape(down_sum.shape[2:]),
    )
    return (
        outputs,
        input_grads,
        mod_grads,
        jnp.stack(qv_grads),
        jnp.stack(out_sums),
        jnp.stack(up_sums),
        jnp.stack(down_sums),
        grads,
    )


def per_device(
    image_tokens,
    text_tokens,
    text_lengths,
    slot_sequence,
    conditioning,
    mod_weight,
    mod_bias,
    qkv_weight,
    qv_bias,
    out_weight,
    out_bias,
    up_weight,
    up_bias,
    down_weight,
    down_bias,
    image_cotan,
    text_cotan,
):
    width = conditioning.shape[1]
    seq_total = conditioning.shape[0]
    image_rows = image_tokens.shape[1]
    text_cap = text_tokens.shape[1]
    owner_rows = mod_weight.shape[0]
    owner_index = lax.axis_index(("shard", "ctx"))
    seq_hot = (jnp.arange(seq_total, dtype=jnp.int32) == slot_sequence[0]).astype(jnp.float32)
    live = (slot_sequence[0] >= 0).astype(jnp.float32)
    text_valid = (jnp.arange(text_cap, dtype=jnp.int32) < text_lengths[0, 0]).astype(jnp.float32)
    row_masks = (jnp.full((image_rows, 1), 1.0, jnp.float32) * live, text_valid[:, None] * live)
    cond_act = jax.nn.silu(conditioning.astype(jnp.float32))
    cond_cols = lax.dynamic_slice_in_dim(
        cond_act.astype(jnp.bfloat16), owner_index * owner_rows, owner_rows, 1
    )
    partial_mod = jnp.einsum(
        "sr,rtm->tsm", cond_cols, mod_weight, preferred_element_type=jnp.float32
    )
    mod_table = lax.psum(partial_mod, ("shard", "ctx")) + mod_bias.astype(jnp.float32)[:, None, :]
    modulation = jnp.sum(seq_hot[None, :, None] * mod_table, axis=1).reshape(2, 6, width)
    inputs = (image_tokens[0].astype(jnp.float32), text_tokens[0].astype(jnp.float32))
    cotangents = (
        image_cotan[0].astype(jnp.float32) * row_masks[0],
        text_cotan[0].astype(jnp.float32) * row_masks[1],
    )
    weights = (qkv_weight, out_weight, up_weight, down_weight)
    biases = (
        qv_bias.astype(jnp.float32),
        out_bias.astype(jnp.float32),
        up_bias.astype(jnp.float32),
        down_bias.astype(jnp.float32),
    )
    result = heads_path(inputs, cotangents, modulation, row_masks, text_valid, weights, biases)
    outputs, input_grads, mod_grads, qv_stack, out_stack, up_stack, down_stack, grads = result
    grad_mod_seq = seq_hot[None, :, None] * jnp.stack(mod_grads)[:, None, :]
    mod_total, qv_total, out_total, up_total, down_total = lax.psum(
        (grad_mod_seq, qv_stack, out_stack, up_stack, down_stack), ("rep", "shard", "ctx")
    )
    qkv_grad, out_grad, up_grad, down_grad = (
        lax.psum(grads[0].astype(jnp.bfloat16), "rep").astype(jnp.float32),
        lax.psum(grads[1].astype(jnp.bfloat16), "rep").astype(jnp.float32),
        lax.psum(grads[2].astype(jnp.bfloat16), "rep").astype(jnp.float32),
        lax.psum(grads[3].astype(jnp.bfloat16), "rep").astype(jnp.float32),
    )
    mod_weight_grad = jnp.einsum(
        "sr,tsm->rtm", cond_cols.astype(jnp.float32), mod_total, precision=lax.Precision.HIGHEST
    )
    mod_bias_grad = owner_slice(jnp.sum(mod_total, axis=1))
    grad_cond_cols = jnp.einsum(
        "tsm,rtm->sr", mod_total, mod_weight.astype(jnp.float32), precision=lax.Precision.HIGHEST
    )
    cond_part = lax.dynamic_slice_in_dim(
        conditioning.astype(jnp.float32), owner_index * owner_rows, owner_rows, 1
    )
    cond_grad = jax.vjp(jax.nn.silu, cond_part)[1](grad_cond_cols)[0]
    return (
        outputs[0],
        outputs[1],
        input_grads[0],
        input_grads[1],
        cond_grad,
        mod_weight_grad,
        mod_bias_grad,
        qkv_grad,
        owner_slice(qv_total),
        out_grad,
        owner_slice(out_total),
        up_grad,
        owner_slice(up_total),
        down_grad,
        owner_slice(down_total),
    )


def solution(mesh):
    return jax.shard_map(
        per_device,
        mesh=mesh,
        in_specs=(
            P(("rep", "shard"), "ctx", None),
            P(("rep", "shard"), "ctx", None),
            P(("rep", "shard"), "ctx"),
            P(("rep", "shard")),
            P(),
            P(("shard", "ctx"), None, None),
            P(),
            P(("shard", "ctx"), None, None),
            P(),
            P(("shard", "ctx"), None, None),
            P(),
            P(("shard", "ctx"), None, None),
            P(),
            P(("shard", "ctx"), None, None),
            P(),
            P(("rep", "shard"), "ctx", None),
            P(("rep", "shard"), "ctx", None),
        ),
        out_specs=(
            P(("rep", "shard"), "ctx", None),
            P(("rep", "shard"), "ctx", None),
            P(("rep", "shard"), "ctx", None),
            P(("rep", "shard"), "ctx", None),
            P(None, ("shard", "ctx")),
            P(("shard", "ctx"), None, None),
            P(None, ("shard", "ctx")),
            P(("shard", "ctx"), None, None),
            P(None, ("shard", "ctx")),
            P(("shard", "ctx"), None, None),
            P(None, ("shard", "ctx")),
            P(("shard", "ctx"), None, None),
            P(None, ("shard", "ctx")),
            P(("shard", "ctx"), None, None),
            P(None, ("shard", "ctx")),
        ),
        check_vma=False,
    )
```

profile of v0, /device:TPU:1, one launch (start us, length us, event | category | flops | bytes accessed | tf_op | source)
XLA Modules:
  0.0 2433.3 jit_solution(7379096680607353550)
XLA Ops:
  14.6 638.8 %all-reduce.9.cloned.1.call-done = f32[2,27,9216]{2,1,0:T(8,128)} async-done(((f32[2,27,9216]{2,1,0:T(8,128)}), f32[2,27,9216]{2,1,0:T(8,128)}) %all-reduce.9.cloned.1.call-update) | async-done | bytes 1990672 | tf_op jit(solution)/shard_map/psum | solution.py:596
  661.8 17.0 reshape.425
  685.6 12.8 all-to-all-done.1
  713.5 68.4 %all-to-all-done = bf16[4,16,24,2,3,384]{5,2,4,3,1,0:T(8,128)(2,1)} async-done(((bf16[4,16,24,2,3,384]{5,2,4,3,1,0:T(8,128)(2,1)}), bf16[4,16,24,2,3,384]{5,2,4,3,1,0:T(8,128)(2,1)}, u32[]{:S(2)}, u32[]{:S(2)}) %all-to-all-start) | async-done | bytes 7077920 | tf_op jit(solution)/shard_map/all_to_all | solution.py:194
  790.0 101.0 %all-reduce.1 = bf16[160]{0:T(256)(128)(2,1)S(1)} all-reduce(bf16[160]{0:T(256)(128)(2,1)S(1)} %dynamic-update-slice), channel_id=1, replica_groups=mesh['rep'=2,'shard'=16,'ctx'=4] {'ctx'}, use_global_device_ids=true, to_apply=%add.1 | all-reduce | flops 160 | bytes 640
  892.2 11.0 all_gather.45
  916.6 18.0 reshape.426
  955.4 23.0 reshape.449
  1020.4 96.8 %all-to-all-done.2 = bf16[4,16,24,2,1,1536]{5,2,1,3,4,0:T(8,128)(2,1)} async-done(((bf16[4,16,24,2,1,1536]{5,2,1,3,4,0:T(8,128)(2,1)}), bf16[4,16,24,2,1,1536]{5,2,1,3,4,0:T(8,128)(2,1)}, u32[]{:S(2)}, u32[]{:S(2)}) %all-to-all-start.2) | async-done | bytes 9437216 | tf_op jit(solution)/shard_map/all_to_all | solution.py:196
  1162.7 12.9 all_gather.51
  1202.6 19.9 reduce-scatter.19.cloned.1.call-done
  1224.1 21.7 reduce-scatter.15.cloned.1.call-done
  1247.8 11.0 all_gather.55
  1261.0 11.7 all-gather.23.cloned.1.call-done
  1330.0 85.2 %all-to-all-done.10 = bf16[4,4,96,2,1536]{4,2,3,1,0:T(8,128)(2,1)} async-done(((bf16[4,4,96,2,1536]{4,2,3,1,0:T(8,128)(2,1)}), bf16[4,4,96,2,1536]{4,2,3,1,0:T(8,128)(2,1)}, u32[]{:S(2)}, u32[]{:S(2)}) %all-to-all-start.10) | async-done | bytes 9437216 | tf_op jit(solution)/shard_map/all_to_all | solution.py:518
  1435.2 86.5 %all-to-all-done.8 = bf16[4,16,24,2,1,1536]{5,2,1,4,3,0:T(8,128)(2,1)} async-done(((bf16[4,16,24,2,1,1536]{5,2,1,4,3,0:T(8,128)(2,1)}), bf16[4,16,24,2,1,1536]{5,2,1,4,3,0:T(8,128)(2,1)}, u32[]{:S(2)}, u32[]{:S(2)}) %all-to-all-start.8) | async-done | bytes 9437216 | tf_op jit(solution)/shard_map/all_to_all | solution.py:515
  1521.7 12.8 all-to-all-start.7
  1582.4 86.6 %all_to_all.80 = bf16[4,16,24,2,3,384]{5,2,4,3,1,0:T(8,128)(2,1)} all-to-all(bf16[4,16,24,2,3,384]{5,2,4,3,1,0:T(8,128)(2,1)} %copy.206), channel_id=1, replica_groups=mesh['rep'=2,'shard'=16,'ctx'=4] {'ctx'}, dimensions={0} | all-to-all | bytes 14155776 | tf_op jit(solution)/shard_map/all_to_all | solution.py:509
  1685.7 140.5 %all-to-all-done.11 = bf16[1,16,96,2,1536]{4,2,3,0,1:T(8,128)(2,1)} async-done(((bf16[1,16,96,2,1536]{4,2,3,0,1:T(8,128)(2,1)}), bf16[1,16,96,2,1536]{4,2,3,0,1:T(8,128)(2,1)}, u32[]{:S(2)}, u32[]{:S(2)}) %all-to-all-start.11) | async-done | bytes 9437216 | tf_op jit(solution)/shard_map/all_to_all | solution.py:534
  1853.7 130.0 %all-to-all-done.9 = bf16[4,16,24,2,1,1536]{5,2,0,4,3,1:T(8,128)(2,1)} async-done(((bf16[4,16,24,2,1,1536]{5,2,0,4,3,1:T(8,128)(2,1)}), bf16[4,16,24,2,1,1536]{5,2,0,4,3,1:T(8,128)(2,1)}, u32[]{:S(2)}, u32[]{:S(2)}) %all-to-all-start.9) | async-done | bytes 9437216 | tf_op jit(solution)/shard_map/all_to_all | solution.py:531
  2016.9 83.4 %all-to-all-done.5 = bf16[4,16,24,2,3,384]{5,2,4,3,0,1:T(8,128)(2,1)} async-done(((bf16[4,16,24,2,3,384]{5,2,4,3,0,1:T(8,128)(2,1)}), bf16[4,16,24,2,3,384]{5,2,4,3,0,1:T(8,128)(2,1)}, u32[]{:S(2)}, u32[]{:S(2)}) %all-to-all-start.5) | async-done | bytes 7077920 | tf_op jit(solution)/shard_map/all_to_all | solution.py:525
  2105.5 93.6 %all-reduce.13.cloned.1.call-done = (f32[2,3072]{1,0:T(2,128)}, f32[2,1536]{1,0:T(2,128)}, f32[2,6144]{1,0:T(2,128)}, f32[2,1536]{1,0:T(2,128)}) async-done(((f32[2,3072]{1,0:T(2,128)}, f32[2,1536]{1,0:T(2,128)}, f32[2,6144]{1,0:T(2,128)}, f32[2,1536]{1,0:T(2,128)}), (f32[2,3072]{1,0:T(2,128)}, f32[2,1536]{1,0:T(2,128)}, f32[2,6144]{1,0:T(2,128)}, f32[2,1536]{1,0:T(2,128)})) %all-reduce.13.cloned.1.call-update) | async-done | bytes 98320 | tf_op jit(solution)/shard_map/psum | solution.py:613
  2203.0 149.1 %all-reduce.11.cloned.1.call-done = f32[2,27,9216]{2,1,0:T(8,128)} async-done(((f32[2,27,9216]{2,1,0:T(8,128)}), f32[2,27,9216]{2,1,0:T(8,128)}) %all-reduce.11.cloned.1.call-update) | async-done | bytes 1990672 | tf_op jit(solution)/shard_map/psum | solution.py:613
  2361.3 56.1 %all-reduce.15.cloned.1.call-done = (bf16[24,2,4608]{2,0,1:T(8,128)(2,1)}, bf16[24,2,1536]{2,0,1:T(8,128)(2,1)}, bf16[24,2,6144]{2,0,1:T(8,128)(2,1)}, bf16[96,2,1536]{2,0,1:T(8,128)(2,1)}) async-done(((bf16[24,2,4608]{2,0,1:T(8,128)(2,1)}, bf16[24,2,1536]{2,0,1:T(8,128)(2,1)}, bf16[24,2,6144]{2,0,1:T(8,128)(2,1)}, bf16[96,2,1536]{2,0,1:T(8,128)(2,1)}), (bf16[24,2,4608]{2,0,1:T(8,128)(2,1)}, ...) | async-done | bytes 1769488 | tf_op jit(solution)/shard_map/psum | solution.py:617
  (460 shorter events, 426.0 us)
Async XLA Ops:
  8.0 645.5 %all-reduce.9.cloned.1.call-start = ((), (), s32[]{:S(2)}) async-start(), calls=%async_computation.20 | async-start | bytes 4718592 | tf_op jit(solution)/shard_map/psum | solution.py:596
  11.3 646.8 %all-gather.13.cloned.1.call-start = ((), (), s32[]{:S(2)}) async-start(), calls=%async_computation.23 | async-start | bytes 2506752 | tf_op jit(solution)/shard_map/all_gather | solution.py:188
  11.9 649.9 %all-gather.11.cloned.1.call-start = ((), (), s32[]{:S(2)}) async-start(), calls=%async_computation.22 | async-start | bytes 7520256 | tf_op jit(solution)/shard_map/all_gather | solution.py:187
  12.5 692.8 %all-gather.19.cloned.1.call-start = ((), (), s32[]{:S(2)}) async-start(), calls=%async_computation.27 | async-start | bytes 10027008 | tf_op jit(solution)/shard_map/all_gather | solution.py:190
  13.5 924.0 %all-gather.9.cloned.1.call-start = ((), (), s32[]{:S(2)}) async-start(), calls=%async_computation.21 | async-start | bytes 1474560 | tf_op jit(solution)/shard_map/all_gather | solution.py:287
  657.3 298.1 %all-gather.17.cloned.1.call-start = ((), (), s32[]{:S(2)}) async-start(), calls=%async_computation.26 | async-start | bytes 10027008 | tf_op jit(solution)/shard_map/all_gather | solution.py:189
  699.9 82.1 %all-to-all-start = ((bf16[4,16,24,2,3,384]{5,2,4,3,1,0:T(8,128)(2,1)}), bf16[4,16,24,2,3,384]{5,2,4,3,1,0:T(8,128)(2,1)}, u32[]{:S(2)}, u32[]{:S(2)}) async-start(bf16[4,16,24,2,3,384]{5,2,4,3,1,0:T(8,128)(2,1)} %bitcast.342), calls=%async_computation | async-start | bytes 14155776 | tf_op jit(solution)/shard_map/all_to_all | solution.py:194
  782.0 215.2 %all-to-all-start.3 = ((bf16[4,384,2,1536]{3,1,2,0:T(8,128)(2,1)}), bf16[4,384,2,1536]{3,1,2,0:T(8,128)(2,1)}, u32[]{:S(2)}, u32[]{:S(2)}) async-start(bf16[4,384,2,1536]{3,1,2,0:T(8,128)(2,1)} %copy.197), calls=%async_computation.4 | async-start | bytes 18874368 | tf_op jit(solution)/shard_map/all_to_all | solution.py:197
  787.8 215.5 %reduce-scatter.9.cloned.1.call-start = ((), (), s32[]{:S(2)}) async-start(), calls=%async_computation.24 | async-start | bytes 1474560 | tf_op jit(solution)/shard_map/reduce_scatter | solution.py:258
  997.2 120.0 %all-to-all-start.2 = ((bf16[4,16,24,2,1,1536]{5,2,1,3,4,0:T(8,128)(2,1)}), bf16[4,16,24,2,1,1536]{5,2,1,3,4,0:T(8,128)(2,1)}, u32[]{:S(2)}, u32[]{:S(2)}) async-start(bf16[4,16,24,2,1,1536]{5,2,1,3,4,0:T(8,128)(2,1)} %copy.194), calls=%async_computation.3 | async-start | bytes 18874368 | tf_op jit(solution)/shard_map/all_to_all | solution.py:196
  1003.2 122.7 %all-gather.15.cloned.1.call-start = ((), (), s32[]{:S(2)}) async-start(), calls=%async_computation.25 | async-start | bytes 1474560 | tf_op jit(solution)/shard_map/all_gather | solution.py:251
  1007.7 124.2 %all-gather.21.cloned.1.call-start = ((), (), s32[]{:S(2)}) async-start(), calls=%async_computation.31 | async-start | bytes 1474560 | tf_op jit(solution)/shard_map/all_gather | solution.py:251
  1009.2 145.3 %reduce-scatter.13.cloned.1.call-start = ((), (), s32[]{:S(2)}) async-start(), calls=%async_computation.29 | async-start | bytes 614400 | tf_op jit(solution)/shard_map/reduce_scatter | solution.py:261
  1012.0 181.0 %reduce-scatter.17.cloned.1.call-start = ((), (), s32[]{:S(2)}) async-start(), calls=%async_computation.32 | async-start | bytes 1474560 | tf_op jit(solution)/shard_map/reduce_scatter | solution.py:258
  1307.9 107.3 %all-to-all-start.10 = ((bf16[4,4,96,2,1536]{4,2,3,1,0:T(8,128)(2,1)}), bf16[4,4,96,2,1536]{4,2,3,1,0:T(8,128)(2,1)}, u32[]{:S(2)}, u32[]{:S(2)}) async-start(bf16[4,4,96,2,1536]{4,2,3,1,0:T(8,128)(2,1)} %copy_bitcast_fusion), calls=%async_computation.18 | async-start | bytes 18874368 | tf_op jit(solution)/shard_map/all_to_all | solution.py:518
  1415.2 106.5 %all-to-all-start.8 = ((bf16[4,16,24,2,1,1536]{5,2,1,4,3,0:T(8,128)(2,1)}), bf16[4,16,24,2,1,1536]{5,2,1,4,3,0:T(8,128)(2,1)}, u32[]{:S(2)}, u32[]{:S(2)}) async-start(bf16[4,16,24,2,1,1536]{5,2,1,4,3,0:T(8,128)(2,1)} %copy_bitcast_fusion.1), calls=%async_computation.16 | async-start | bytes 18874368 | tf_op jit(solution)/shard_map/all_to_all | solution.py:515
  1669.1 157.2 %all-to-all-start.11 = ((bf16[1,16,96,2,1536]{4,2,3,0,1:T(8,128)(2,1)}), bf16[1,16,96,2,1536]{4,2,3,0,1:T(8,128)(2,1)}, u32[]{:S(2)}, u32[]{:S(2)}) async-start(bf16[1,16,96,2,1536]{4,2,3,0,1:T(8,128)(2,1)} %bitcast.81), calls=%async_computation.19 | async-start | bytes 18874368 | tf_op jit(solution)/shard_map/all_to_all | solution.py:534
  1826.3 157.4 %all-to-all-start.9 = ((bf16[4,16,24,2,1,1536]{5,2,0,4,3,1:T(8,128)(2,1)}), bf16[4,16,24,2,1,1536]{5,2,0,4,3,1:T(8,128)(2,1)}, u32[]{:S(2)}, u32[]{:S(2)}) async-start(bf16[4,16,24,2,1,1536]{5,2,0,4,3,1:T(8,128)(2,1)} %copy.216), calls=%async_computation.17 | async-start | bytes 18874368 | tf_op jit(solution)/shard_map/all_to_all | solution.py:531
  1834.5 158.2 %reduce-scatter.23.cloned.1.call-start = ((), (), s32[]{:S(2)}) async-start(), calls=%async_computation.36 | async-start | bytes 614400 | tf_op jit(solution)/shard_map/reduce_scatter | solution.py:261
  1838.8 157.1 %reduce-scatter.21.cloned.1.call-start = ((), (), s32[]{:S(2)}) async-start(), calls=%async_computation.35 | async-start | bytes 1474560 | tf_op jit(solution)/shard_map/reduce_scatter | solution.py:258
  1983.7 116.6 %all-to-all-start.5 = ((bf16[4,16,24,2,3,384]{5,2,4,3,0,1:T(8,128)(2,1)}), bf16[4,16,24,2,3,384]{5,2,4,3,0,1:T(8,128)(2,1)}, u32[]{:S(2)}, u32[]{:S(2)}) async-start(bf16[4,16,24,2,3,384]{5,2,4,3,0,1:T(8,128)(2,1)} %copy.207), calls=%async_computation.13 | async-start | bytes 14155776 | tf_op jit(solution)/shard_map/all_to_all | solution.py:525
  1991.9 207.1 %all-reduce.13.cloned.1.call-start = ((), (), s32[]{:S(2)}) async-start(), calls=%async_computation.38 | async-start | bytes 196608 | tf_op jit(solution)/shard_map/psum | solution.py:613
  1992.7 359.4 %all-reduce.11.cloned.1.call-start = ((), (), s32[]{:S(2)}) async-start(), calls=%async_computation.37 | async-start | bytes 4718592 | tf_op jit(solution)/shard_map/psum | solution.py:613
  2001.3 416.1 %all-reduce.15.cloned.1.call-start = ((), (), s32[]{:S(2)}) async-start(), calls=%async_computation.39 | async-start | bytes 3538944 | tf_op jit(solution)/shard_map/psum | solution.py:617
  (108 other events, 4994.2 us)
Sparse Core Ops, SparseCore 0:
  11.5 641.9 all-reduce.8
  1999.7 199.3 all-reduce.12
  2203.8 148.1 all-reduce.10
  2355.9 61.3 all-reduce.14
Sparse Core Ops, SparseCore 1:
  14.5 53.2 all-gather.12
  70.3 66.7 all-gather.10
  140.2 76.0 all-gather.18
  657.4 30.4 all-gather.8
  690.6 82.1 all-gather.16
  955.5 23.6 reduce-scatter.8
  1007.8 36.2 all-gather.14
  1046.2 75.2 all-gather.20
  1124.5 19.3 reduce-scatter.12
  1146.9 26.6 reduce-scatter.16
  1176.4 22.8 reduce-scatter.10
  1202.3 20.1 reduce-scatter.18
  1224.9 20.9 reduce-scatter.14
  1248.1 24.5 all-gather.22
  1838.8 18.6 reduce-scatter.22
  1860.7 23.8 reduce-scatter.20
where the time goes:
time: 2440 us; the launch traced here: 2430 us
  waiting for transfers between devices  1710 us (70%)
  blocking collectives  233 us (10%)
  local copies, waits for them, and re-layouts  197 us (8%)
  matrix products  111 us (5%)
  other arithmetic  87.8 us (4%)
  starting transfers between devices  75.5 us (3%)
    psum x1, waiting for transfers between devices, per_device(): lax.psum(partial_mod, ('shard', 'ctx'))  639 us
    psum x2, waiting for transfers between devices, per_device(): lax.psum((grad_mod_seq, qv_stack, out_stack, up_stack, down_stack), ('rep...  243 us
    all_to_all x1, waiting for transfers between devices, heads_path(): lax.all_to_all(down_got.astype(jnp.bfloat16), 'shard', split_axis=1, conc...  141 us
    all_to_all x1, waiting for transfers between devices, heads_path(): lax.all_to_all(up_got.astype(jnp.bfloat16), 'shard', split_axis=1, concat...  130 us
    unnamed x1, blocking collectives  101 us
    all_to_all x1, waiting for transfers between devices, slice_weights(): lax.all_to_all(up_send, 'ctx', split_axis=0, concat_axis=0, tiled=True)  96.8 us
    all_to_all x1, blocking collectives, heads_path(): lax.all_to_all(qkv_send.astype(jnp.bfloat16), 'ctx', split_axis=0, concat...  86.6 us
    all_to_all x1, waiting for transfers between devices, heads_path(): lax.all_to_all(up_send.astype(jnp.bfloat16), 'ctx', split_axis=0, concat_...  86.5 us
  transfers between devices with their start and end apart: 31, of which 17 were waited for; matrix products, arithmetic and copies ran while one was open for 15% of the time, Pallas kernels for 0%

commit v1 on v0

v1 whole, which is shorter than its diff:
```python
import jax
import jax.numpy as jnp
from jax import lax
from jax.sharding import Mesh, PartitionSpec as P

HEAD_DIM = 64
SHARD = ("y", "zh", "core")
OWNER = ("y", "zh", "core", "ctx")
SLOT = ("rep", "y", "zh", "core")
EVERY = ("rep", "y", "zh", "core", "ctx")
BF = jnp.bfloat16
F32 = jnp.float32


def norm_rows(values):
    center = values - jnp.mean(values, axis=-1, keepdims=True)
    inv_scale = lax.rsqrt(jnp.mean(center * center, axis=-1, keepdims=True) + 1e-06)
    return (center * inv_scale, inv_scale)


def norm_back(grad_out, normed, inv_scale):
    return inv_scale * (
        grad_out
        - jnp.mean(grad_out, axis=-1, keepdims=True)
        - normed * jnp.mean(grad_out * normed, axis=-1, keepdims=True)
    )


def gelu_tanh(values):
    return jax.nn.gelu(values, approximate=True)


def mm(left, right):
    return jnp.dot(left, right, preferred_element_type=F32)


def mm_nt(left, right):
    return lax.dot_general(left, right, (((1,), (1,)), ((), ())), preferred_element_type=F32)


def mm_tn(left, right):
    return lax.dot_general(left, right, (((0,), (0,)), ((), ())), preferred_element_type=F32)


def split_heads(matrix):
    return matrix.reshape(matrix.shape[0], -1, HEAD_DIM)


def joint_scores(query, all_keys, all_bias):
    scores = jnp.einsum(
        "qhd,khd->hqk", split_heads(query), split_heads(all_keys), preferred_element_type=F32
    )
    return scores * 0.125 + all_bias[None, None, :]


def attention_forward(query, all_keys, all_values, all_bias):
    scores = joint_scores(query, all_keys, all_bias)
    top_score = jnp.max(scores, axis=-1, keepdims=True)
    exp_scores = jnp.exp(scores - top_score)
    row_total = jnp.sum(exp_scores, axis=-1, keepdims=True)
    log_total = top_score + jnp.log(row_total)
    weights = (exp_scores / row_total).astype(BF)
    mixed = jnp.einsum("hqk,khd->qhd", weights, split_heads(all_values), preferred_element_type=F32)
    return (mixed.reshape(query.shape).astype(BF), log_total)


def attention_backward(query, all_keys, all_values, all_bias, log_total, grad_mixed):
    grad_heads = split_heads(grad_mixed)
    probs = jnp.exp(joint_scores(query, all_keys, all_bias) - log_total)
    grad_probs = jnp.einsum(
        "qhd,khd->hqk", grad_heads, split_heads(all_values), preferred_element_type=F32
    )
    delta = jnp.sum(probs * grad_probs, axis=-1, keepdims=True)
    grad_scores = (probs * (grad_probs - delta)).astype(BF)
    grad_query = (
        jnp.einsum("hqk,khd->qhd", grad_scores, split_heads(all_keys), preferred_element_type=F32)
        * 0.125
    )
    grad_keys = (
        jnp.einsum("hqk,qhd->khd", grad_scores, split_heads(query), preferred_element_type=F32)
        * 0.125
    )
    grad_values = jnp.einsum(
        "hqk,qhd->khd", probs.astype(BF), grad_heads, preferred_element_type=F32
    )
    return tuple(g.reshape(query.shape).astype(BF) for g in (grad_query, grad_keys, grad_values))


def turn(values, axis, step):
    count = lax.axis_size(axis)
    return lax.ppermute(values, axis, [(i, (i + step) % count) for i in range(count)])


def ring_gather(block):
    half = block.shape[0] // 2 // 8 * 8
    behind = turn(block, "ctx", 1)
    ahead = turn(block, "ctx", -1)
    far_top = turn(behind[:half], "ctx", 1)
    far_bottom = turn(ahead[half:], "ctx", -1)
    return [block, ahead, jnp.concatenate([far_top, far_bottom]), behind]


def ring_scatter(blocks):
    half = blocks[0].shape[0] // 2 // 8 * 8
    from_behind = turn(blocks[2][:half], "ctx", 1)
    from_ahead = turn(blocks[2][half:], "ctx", -1)
    to_ahead = jnp.concatenate([blocks[1][:half] + from_behind, blocks[1][half:]])
    to_behind = jnp.concatenate([blocks[3][:half], blocks[3][half:] + from_ahead])
    got_behind = turn(to_ahead, "ctx", 1)
    got_ahead = turn(to_behind, "ctx", -1)
    return blocks[0].astype(F32) + got_behind.astype(F32) + got_ahead.astype(F32)


def direct_gather(block, axis):
    return [block] + [turn(block, axis, -k) for k in range(1, lax.axis_size(axis))]


def split_streams(blocks, image_rows, rows):
    return (
        jnp.concatenate([b[:image_rows] for b in blocks]),
        jnp.concatenate([b[image_rows:rows] for b in blocks]),
    )


def join_streams(image, text):
    image_rows, text_rows = image.shape[0] // 4, text.shape[0] // 4
    return [
        jnp.concatenate(
            [
                image[k * image_rows : (k + 1) * image_rows],
                text[k * text_rows : (k + 1) * text_rows],
            ]
        )
        for k in range(4)
    ]


def per_device(
    image_tokens,
    text_tokens,
    text_lengths,
    slot_sequence,
    conditioning,
    mod_weight,
    mod_bias,
    qkv_weight,
    qv_bias,
    out_weight,
    out_bias,
    up_weight,
    up_bias,
    down_weight,
    down_bias,
    image_cotan,
    text_cotan,
):
    seq_total, width = conditioning.shape
    image_rows, text_cap = image_tokens.shape[1], text_tokens.shape[1]
    rows = image_rows + text_cap
    own_rows = mod_weight.shape[0]
    span, ff = width // 4, up_weight.shape[2]
    ff_span = ff // 4
    position = lax.axis_index("ctx")
    owner_index = lax.axis_index(OWNER)
    shards = 16

    meta = jnp.broadcast_to(text_lengths[0, 0].astype(BF), (8, width))
    token_blocks = ring_gather(jnp.concatenate([image_tokens[0], text_tokens[0], meta]))
    image_all, text_all = split_streams(token_blocks, image_rows, rows)
    lengths = [b[rows, 0].astype(F32) for b in token_blocks]
    cotan_blocks = ring_gather(jnp.concatenate([image_cotan[0], text_cotan[0]]))
    image_cot_all, text_cot_all = split_streams(cotan_blocks, image_rows, rows)

    col_send = jnp.concatenate(
        [
            qkv_weight.reshape(own_rows, 2, 3, 4, span)
            .transpose(3, 1, 0, 2, 4)
            .reshape(4, 2, own_rows, 3 * span),
            up_weight.reshape(own_rows, 2, 4, ff_span).transpose(2, 1, 0, 3),
        ],
        axis=3,
    )
    col_got = lax.all_to_all(col_send, "ctx", split_axis=0, concat_axis=0, tiled=True)
    col_got = col_got.transpose(1, 0, 2, 3).reshape(2, 4 * own_rows, -1)
    to_slice = [(b, (b % shards) * 4 + b // shards) for b in range(4 * shards)]
    from_slice = [(d, s) for s, d in to_slice]
    row_send = jnp.concatenate([out_weight, down_weight]).transpose(1, 0, 2)
    row_got = lax.ppermute(row_send, OWNER, to_slice)

    def gather_rows(values):
        return lax.all_gather(values, SHARD, axis=0, tiled=True)

    qkv_cols = [gather_rows(col_got[t, :, : 3 * span]) for t in range(2)]
    out_rows = [gather_rows(row_got[t, :own_rows]) for t in range(2)]
    up_cols = [gather_rows(col_got[t, :, 3 * span :]) for t in range(2)]
    down_rows = [gather_rows(row_got[t, own_rows:]) for t in range(2)]

    all_sequences = lax.all_gather(slot_sequence, SLOT, axis=0, tiled=True)
    slot_hot = (
        all_sequences[:, None] == jnp.arange(seq_total, dtype=jnp.int32)[None, :]
    ).astype(F32)
    live = (slot_sequence[0] >= 0).astype(F32)
    cond_float = conditioning.astype(F32)
    cond_cols = lax.dynamic_slice_in_dim(
        jax.nn.silu(cond_float).astype(BF), owner_index * own_rows, own_rows, 1
    )
    slot_cond = mm(slot_hot.astype(BF), cond_cols).astype(BF)
    my_cond = lax.dynamic_slice_in_dim(slot_cond, lax.axis_index("rep") * shards, shards, 0)
    mod_matrix = mod_weight.reshape(own_rows, -1)
    partial_mod = mm(my_cond, mod_matrix).astype(BF)
    got_mod = lax.all_to_all(partial_mod, SHARD, split_axis=0, concat_axis=0, tiled=True)
    slot_mod = jnp.sum(got_mod.astype(F32), axis=0).astype(BF).reshape(8, -1)
    all_mod = direct_gather(slot_mod, "ctx")
    modulation = (
        sum(m.astype(F32) for m in all_mod).reshape(2, 6, width)
        + mod_bias.astype(F32).reshape(2, 6, width)
    ) * live

    own_masks = (
        jnp.full((image_rows, 1), 1.0, F32) * live,
        (jnp.arange(text_cap, dtype=jnp.int32) < text_lengths[0, 0]).astype(F32)[:, None] * live,
    )
    row_mask = jnp.concatenate(own_masks)
    text_valid = jnp.concatenate(
        [(jnp.arange(text_cap, dtype=jnp.int32).astype(F32) < n).astype(F32) for n in lengths]
    )
    key_bias = jnp.concatenate(
        [jnp.zeros((4 * image_rows,), F32), (text_valid - 1.0) * 1000000000.0]
    )
    bias_at = lambda values, start, size: lax.dynamic_slice_in_dim(values, start, size, 1)
    q_bias = bias_at(qv_bias, position * span, span).astype(F32)
    v_bias = bias_at(qv_bias, width + position * span, span).astype(F32)
    up_part = bias_at(up_bias, position * ff_span, ff_span).astype(F32)
    normed_first, modulated_first, queries, keys, values = ([], [], [], [], [])
    for t, tokens in enumerate((image_all, text_all)):
        normed, _ = norm_rows(tokens.astype(F32))
        modulated = (normed * (1.0 + modulation[t, 1]) + modulation[t, 0]).astype(BF)
        projected = mm(modulated, qkv_cols[t])
        queries.append((projected[:, :span] + q_bias[t]).astype(BF))
        keys.append(projected[:, span : 2 * span].astype(BF))
        values.append((projected[:, 2 * span :] + v_bias[t]).astype(BF))
        normed_first.append(normed)
        modulated_first.append(modulated)
    query, all_keys, all_values = (jnp.concatenate(v) for v in (queries, keys, values))
    mixed, log_total = attention_forward(query, all_keys, all_values, key_bias)
    count = 4 * image_rows
    mixed_parts = (mixed[:count], mixed[count:])
    attn = ring_scatter(
        join_streams(*(mm(mixed_parts[t], out_rows[t]).astype(BF) for t in range(2)))
    )

    def both(at, plus=0.0):
        return jnp.concatenate(
            [
                jnp.broadcast_to(plus + modulation[0, at], (image_rows, width)),
                jnp.broadcast_to(plus + modulation[1, at], (text_cap, width)),
            ]
        )

    def spread(vectors):
        return jnp.concatenate(
            [
                jnp.broadcast_to(vectors[0], (image_rows, width)),
                jnp.broadcast_to(vectors[1], (text_cap, width)),
            ]
        )

    def sums(matrix):
        return jnp.stack([jnp.sum(matrix[:image_rows], 0), jnp.sum(matrix[image_rows:], 0)])

    tokens = jnp.concatenate([image_tokens[0], text_tokens[0]]).astype(F32)
    own_cotan = jnp.concatenate([image_cotan[0], text_cotan[0]]).astype(F32) * row_mask
    attn = attn + spread(out_bias.astype(F32))
    middle = tokens + both(2) * attn
    normed_two, inv_two = norm_rows(middle)
    modulated_two = (normed_two * both(4, 1.0) + both(3)).astype(BF)

    seconds = split_streams(ring_gather(modulated_two), image_rows, rows)
    branch_grads = (
        (image_cot_all.astype(F32) * live * modulation[0, 5]).astype(BF),
        (text_cot_all.astype(F32) * (text_valid * live)[:, None] * modulation[1, 5]).astype(BF),
    )
    actives, hidden_grads, down_parts, second_parts = ([], [], [], [])
    for t in range(2):
        hidden = mm(seconds[t], up_cols[t]) + up_part[t]
        activated, pull = jax.vjp(gelu_tanh, hidden)
        actives.append(activated.astype(BF))
        grad_active = mm_nt(branch_grads[t], down_rows[t])
        hidden_grads.append(pull(grad_active)[0].astype(BF))
        second_parts.append(mm_nt(hidden_grads[t], up_cols[t]).astype(BF))
        down_parts.append(mm(actives[t], down_rows[t]).astype(BF))
    grad_two = ring_scatter(join_streams(*second_parts))
    grad_middle = own_cotan + norm_back(grad_two * both(4, 1.0), normed_two, inv_two)
    grad_attn = (grad_middle * both(2)).astype(BF)
    attn_grads = split_streams(ring_gather(grad_attn), image_rows, rows)

    branch = ring_scatter(join_streams(*down_parts)) + spread(down_bias.astype(F32))
    outs = ((middle + both(5) * branch) * row_mask).astype(BF)
    grad_gate_two = sums(own_cotan * branch)

    def scatter_rows(values):
        return lax.psum_scatter(values, SHARD, scatter_dimension=0, tiled=True)

    down_own = [scatter_rows(mm_tn(actives[t], branch_grads[t]).astype(BF)) for t in range(2)]
    up_own = [scatter_rows(mm_tn(seconds[t], hidden_grads[t]).astype(BF)) for t in range(2)]

    grad_mixed = jnp.concatenate([mm_nt(attn_grads[t], out_rows[t]).astype(BF) for t in range(2)])
    out_own = [scatter_rows(mm_tn(mixed_parts[t], attn_grads[t]).astype(BF)) for t in range(2)]
    grad_qkv = attention_backward(query, all_keys, all_values, key_bias, log_total, grad_mixed)
    grad_qkv = jnp.concatenate(grad_qkv, axis=1)
    proj_grads = (grad_qkv[:count], grad_qkv[count:])
    first_parts = [mm_nt(proj_grads[t], qkv_cols[t]) for t in range(2)]
    grad_one = ring_scatter(join_streams(*(f.astype(BF) for f in first_parts)))
    qkv_own = [scatter_rows(mm_tn(modulated_first[t], proj_grads[t]).astype(BF)) for t in range(2)]

    normed_one, inv_one = norm_rows(tokens)
    input_grad = grad_middle + norm_back(grad_one * both(1, 1.0), normed_one, inv_one)

    vectors = jnp.stack(
        [
            jnp.stack([jnp.sum(f, 0) for f in first_parts]),
            jnp.stack([jnp.sum(f * n, 0) for f, n in zip(first_parts, normed_first)]),
            sums(grad_middle * attn),
            sums(grad_two),
            sums(grad_two * normed_two),
            grad_gate_two,
            sums(grad_attn.astype(F32)),
            sums(own_cotan * both(5)),
        ],
        axis=1,
    )
    vectors = vectors.reshape(2, 8, 4, span).transpose(2, 0, 1, 3).reshape(4, 2 * 8 * span)
    vectors = jnp.sum(
        lax.all_to_all(vectors, "ctx", split_axis=0, concat_axis=0, tiled=True), axis=0
    )
    qv_sums = jnp.stack([jnp.sum(g.astype(F32), 0) for g in proj_grads]).reshape(2, 3, span)
    up_sums = jnp.stack([jnp.sum(g.astype(F32), 0) for g in hidden_grads])
    own_vector = jnp.concatenate(
        [vectors, qv_sums[:, 0].reshape(-1), qv_sums[:, 2].reshape(-1), up_sums.reshape(-1)]
    ).astype(BF)
    size = own_vector.shape[0]
    gathered = own_vector.reshape(1, 1, 1, 1, 4, size // 4)
    for axis, name in ((3, "ctx"), (1, "y")):
        here = lax.axis_index(name)
        blocks = jnp.concatenate(direct_gather(gathered, name), axis=axis)
        gathered = jnp.roll(blocks, here, axis=axis)
    for axis, name in ((0, "rep"), (2, "zh")):
        here = lax.axis_index(name)
        other = turn(gathered, name, 1)
        gathered = jnp.where(
            here == 0,
            jnp.concatenate([gathered, other], axis),
            jnp.concatenate([other, gathered], axis),
        )
    other = turn(gathered, "core", 1)
    gathered = jnp.stack([gathered, other], axis=3)
    gathered = jnp.where(lax.axis_index("core") == 0, gathered, gathered[:, :, :, ::-1])
    everything = gathered.reshape(2 * shards, 4, size)
    slots = 2 * shards
    vec_size = 2 * 8 * span
    table = everything[:, :, :vec_size].reshape(slots, 4, 2, 8, span).transpose(0, 2, 3, 1, 4)
    table = table.reshape(slots, 2, 8, width)
    slot_live = (all_sequences >= 0).astype(BF)[:, None, None, None]
    mod_rows = (table[:, :, :6] * slot_live).reshape(slots, -1)
    mod_weight_grad = mm_tn(slot_cond, mod_rows).reshape(mod_weight.shape)

    def owner_slice(values):
        part = values.shape[1] // (4 * shards)
        return lax.dynamic_slice_in_dim(values, owner_index * part, part, 1)

    mod_bias_grad = owner_slice(jnp.sum(mod_rows.astype(F32), 0).reshape(2, -1))
    out_bias_grad = owner_slice(jnp.sum(table[:, :, 6].astype(F32), 0))
    down_bias_grad = owner_slice(jnp.sum(table[:, :, 7].astype(F32), 0))
    rest = jnp.sum(everything[:, :, vec_size:].astype(F32), 0)
    q_total, v_total, up_total = (
        rest[:, a:b].reshape(4, 2, -1).transpose(1, 0, 2).reshape(2, -1)
        for a, b in ((0, 2 * span), (2 * span, 4 * span), (4 * span, 4 * span + 2 * ff_span))
    )
    qv_bias_grad = owner_slice(jnp.concatenate([q_total, v_total], axis=1))
    up_bias_grad = owner_slice(up_total)
    slot_grads = mm_nt(mod_rows, mod_matrix)
    grad_cond_cols = lax.dot_general(
        slot_hot, slot_grads, (((0,), (0,)), ((), ())), precision=lax.Precision.HIGHEST
    )
    cond_part = lax.dynamic_slice_in_dim(cond_float, owner_index * own_rows, own_rows, 1)
    cond_grad = jax.vjp(jax.nn.silu, cond_part)[1](grad_cond_cols)[0]

    col_back = jnp.stack(
        [
            jnp.concatenate([qkv_own[t], up_own[t]], axis=1).reshape(4, own_rows, -1)
            for t in range(2)
        ],
        axis=2,
    )
    col_back = lax.all_to_all(col_back, "ctx", split_axis=0, concat_axis=0, tiled=True)
    row_back = jnp.stack(
        [jnp.concatenate([out_own[t], down_own[t]]) for t in range(2)], axis=1
    )
    row_back = lax.ppermute(row_back, OWNER, from_slice)
    col_back = col_back.astype(F32) + turn(col_back, "rep", 1).astype(F32)
    row_back = row_back.astype(F32) + turn(row_back, "rep", 1).astype(F32)
    qkv_grad = (
        col_back[..., : 3 * span]
        .reshape(4, own_rows, 2, 3, span)
        .transpose(1, 2, 3, 0, 4)
        .reshape(qkv_weight.shape)
    )
    up_grad = col_back[..., 3 * span :].transpose(1, 2, 0, 3).reshape(up_weight.shape)
    out_grad, down_grad = (row_back[:own_rows], row_back[own_rows:])
    return (
        outs[None, :image_rows],
        outs[None, image_rows:],
        input_grad[None, :image_rows],
        input_grad[None, image_rows:],
        cond_grad,
        mod_weight_grad,
        mod_bias_grad,
        qkv_grad,
        qv_bias_grad,
        out_grad,
        out_bias_grad,
        up_grad,
        up_bias_grad,
        down_grad,
        down_bias_grad,
    )


def solution(mesh):
    fine = Mesh(mesh.devices.reshape(2, 4, 2, 2, 4), EVERY)
    rows = P(SLOT, "ctx", None)
    owned = P(OWNER, None, None)
    columns = P(None, OWNER)
    return jax.shard_map(
        per_device,
        mesh=fine,
        in_specs=(
            rows,
            rows,
            P(SLOT, "ctx"),
            P(SLOT),
            P(),
            owned,
            P(),
            owned,
            P(),
            owned,
            P(),
            owned,
            P(),
            owned,
            P(),
            rows,
            rows,
        ),
        out_specs=(
            rows,
            rows,
            rows,
            rows,
            columns,
            owned,
            columns,
            owned,
            columns,
            owned,
            columns,
            owned,
            columns,
            owned,
            columns,
        ),
        check_vma=False,
    )
```

time: 2440 us -> 1260 us (0.52)
  waiting for transfers between devices: 1710 us -> 818 us
  blocking collectives: 233 us -> 35.3 us
  local copies, waits for them, and re-layouts: 197 us -> 93 us
  starting transfers between devices: 75.5 us -> 101 us
    psum x4 -> x0, waiting for transfers between devices: 938 us -> none  [the longest x1 639 us: per_device(): lax.psum(partial_mod, ('shard', 'ctx'))]
    all_to_all x11 -> x3, waiting for transfers between devices: 712 us -> 21.7 us  [the longest x1 9.34 us: per_device(): lax.all_to_all(col_back, 'ctx', split_axis=0, concat_axis=0, tiled=True)]
    reduce_scatter x8, waiting for transfers between devices: 45.9 us -> 425 us  [scatter_rows(): return lax.psum_scatter(values, SHARD, scatter_dimension=0, tiled=True)]
    all_gather x8, waiting for transfers between devices: 11.8 us -> 249 us  [gather_rows(): return lax.all_gather(values, SHARD, axis=0, tiled=True)]
    ppermute x0 -> x48, waiting for transfers between devices: none -> 120 us  [the longest x46 85.4 us: turn(): lax.ppermute(values, axis, [(i, (i + step) % count) for i in range(count)])]
    unnamed x1, blocking collectives: 101 us -> 16.5 us
    ppermute x0 -> x48, starting transfers between devices: none -> 80.8 us  [the longest x46 70.9 us: turn(): lax.ppermute(values, axis, [(i, (i + step) % count) for i in range(count)])]
    reshape x7 -> x18, local copies, waits for them, and re-layouts: 86.1 us -> 13.6 us  [the longest x1 3.84 us: per_device(): mod_rows = (table[:, :, :6] * slot_live).reshape(slots, -1)]
  transfers between devices with their start and end apart: 31 -> 67, of which waited for: 17 -> 34; matrix products, arithmetic and copies ran while one was open for 15% -> 19% of each run, Pallas kernels for 0% -> 0%
where the time goes in v1:
time: 1260 us; the launch traced here: 1250 us
  waiting for transfers between devices  818 us (65%)
  matrix products  110 us (9%)
  starting transfers between devices  101 us (8%)
  local copies, waits for them, and re-layouts  93 us (7%)
  other arithmetic  71.5 us (6%)
  blocking collectives  35.3 us (3%)
  between operations  20.6 us (2%)
    reduce_scatter x8, waiting for transfers between devices, scatter_rows(): return lax.psum_scatter(values, SHARD, scatter_dimension=0, tiled=True)  425 us
    all_gather x8, waiting for transfers between devices, gather_rows(): return lax.all_gather(values, SHARD, axis=0, tiled=True)  249 us
    ppermute x46, waiting for transfers between devices, turn(): lax.ppermute(values, axis, [(i, (i + step) % count) for i in range(count)])  85.4 us
    ppermute x46, starting transfers between devices, turn(): lax.ppermute(values, axis, [(i, (i + step) % count) for i in range(count)])  70.9 us
    dot_general x9, matrix products, mm_tn(): lax.dot_general(left, right, (((0,), (0,)), ((), ())), preferred_element_...  35 us
    ppermute x1, waiting for transfers between devices, per_device(): row_got = lax.ppermute(row_send, OWNER, to_slice)  34.6 us
    dot_general x9, matrix products, mm_nt(): lax.dot_general(left, right, (((1,), (1,)), ((), ())), preferred_element_...  30.9 us
    dot_general x10, matrix products, mm(): return jnp.dot(left, right, preferred_element_type=F32)  30.3 us
  transfers between devices with their start and end apart: 67, of which 34 were waited for; matrix products, arithmetic and copies ran while one was open for 19% of the time, Pallas kernels for 0%

profile of v1, /device:TPU:1, one launch (start us, length us, event | category | flops | bytes accessed | tf_op | source)
XLA Modules:
  0.0 1250.0 jit_solution(3020505312593605414)
XLA Ops:
  10.6 18.8 %all_to_all.29 = bf16[4,2,24,2688]{3,2,1,0:T(8,128)(2,1)S(1)} all-to-all(bf16[4,2,24,2688]{3,2,1,0:T(8,128)(2,1)S(1)} %copy.191), channel_id=1, replica_groups=mesh['rep'=2,'y'=4,'zh'=2,'core'=2,'ctx'=4] {'ctx'}, dimensions={0} | all-to-all | bytes 2064384 | tf_op jit(solution)/shard_map/all_to_all | solution.py:183
  36.3 34.6 %collective-permute-done.7 = bf16[2,120,1536]{2,1,0:T(8,128)(2,1)S(1)} collective-permute-done((bf16[2,120,1536]{2,1,0:T(8,128)(2,1)S(1)}, bf16[2,120,1536]{2,1,0:T(8,128)(2,1)S(1)}, u32[]{:S(2)}, u32[]{:S(2)}) %collective-permute-start.7) | collective-permute-done | bytes 737312 | tf_op jit(solution)/shard_map/ppermute | solution.py:188
  81.5 16.5 %all-reduce.2 = s32[32]{0:T(128)S(1)} all-reduce(s32[32]{0:T(128)S(1)} %dynamic-update-slice), channel_id=1, replica_groups=mesh['rep'=2,'y'=4,'zh'=2,'core'=2,'ctx'=4] {'rep','y','zh','core'}, use_global_device_ids=true, to_apply=%add.2 | all-reduce | flops 32 | bytes 256
  101.8 10.1 all-to-all-start
  116.6 8.5 all-to-all-done
  143.9 15.4 %all-gather.17.cloned.1.call-done = bf16[1,1536,1152]{2,1,0:T(8,128)(2,1)} async-done(((bf16[1,96,1152]{2,1,0:T(8,128)(2,1)}), bf16[1,1536,1152]{2,1,0:T(8,128)(2,1)}) %all-gather.17.cloned.1.call-update) | async-done | bytes 3538960 | tf_op jit(solution)/shard_map/all_gather | solution.py:191
  173.5 33.0 %all-gather.21.cloned.1.call-done = bf16[1,384,1536]{2,1,0:T(8,128)(2,1)} async-done(((bf16[1,24,1536]{2,1,0:T(8,128)(2,1)}), bf16[1,384,1536]{2,1,0:T(8,128)(2,1)}) %all-gather.21.cloned.1.call-update) | async-done | bytes 1179664 | tf_op jit(solution)/shard_map/all_gather | solution.py:191
  209.9 43.1 %all-gather.23.cloned.1.call-done = bf16[1,384,1536]{2,1,0:T(8,128)(2,1)} async-done(((bf16[1,24,1536]{2,1,0:T(8,128)(2,1)}), bf16[1,384,1536]{2,1,0:T(8,128)(2,1)}) %all-gather.23.cloned.1.call-update) | async-done | bytes 1179664 | tf_op jit(solution)/shard_map/all_gather | solution.py:191
  318.0 53.3 %all-gather.27.cloned.1.call-done = bf16[1,1536,1536]{2,1,0:T(8,128)(2,1)} async-done(((bf16[1,96,1536]{2,1,0:T(8,128)(2,1)}), bf16[1,1536,1536]{2,1,0:T(8,128)(2,1)}) %all-gather.27.cloned.1.call-update) | async-done | bytes 4718608 | tf_op jit(solution)/shard_map/all_gather | solution.py:191
  371.3 7.3 fusion.212
  382.4 48.0 %all-gather.29.cloned.1.call-done = bf16[1,1536,1536]{2,1,0:T(8,128)(2,1)} async-done(((bf16[1,96,1536]{2,1,0:T(8,128)(2,1)}), bf16[1,1536,1536]{2,1,0:T(8,128)(2,1)}) %all-gather.29.cloned.1.call-update) | async-done | bytes 4718608 | tf_op jit(solution)/shard_map/all_gather | solution.py:191
  435.6 54.4 %all-gather.31.cloned.1.call-done = bf16[1,1536,1536]{2,1,0:T(8,128)(2,1)} async-done(((bf16[1,96,1536]{2,1,0:T(8,128)(2,1)}), bf16[1,1536,1536]{2,1,0:T(8,128)(2,1)}) %all-gather.31.cloned.1.call-update) | async-done | bytes 4718608 | tf_op jit(solution)/shard_map/all_gather | solution.py:191
  511.1 8.3 collective-permute-done.25
  546.7 7.0 convolution_convert_fusion.1
  701.6 12.2 collective-permute-done.43
  715.0 14.1 %collective-permute-start.44 = (bf16[2,4,2,4,4,2688]{5,4,2,1,0,3:T(4,128)(2,1)S(1)}, bf16[2,4,2,4,4,2688]{5,4,2,1,0,3:T(4,128)(2,1)S(1)}, u32[]{:S(2)}, u32[]{:S(2)}) collective-permute-start(bf16[2,4,2,4,4,2688]{5,4,2,1,0,3:T(4,128)(2,1)S(1)} %maximum_select_fusion.1), channel_id=1, source_target_pairs={{0,4},{4,0},{1,5},{5,1},{2,6},{6,2},{3,7},{7,3},{8,12},{12,8},{9,1... | collective-permute-start | bytes 4128776 | tf_op jit(solution)/shard_map/ppermute | solution.py:91
  752.9 15.7 %reduce-scatter.21.cloned.1.call-done = bf16[24,1536]{1,0:T(8,128)(2,1)} async-done(((bf16[384,1536]{1,0:T(8,128)(2,1)}), bf16[24,1536]{1,0:T(8,128)(2,1)}) %reduce-scatter.21.cloned.1.call-update) | async-done | bytes 73744 | tf_op jit(solution)/shard_map/reduce_scatter | solution.py:302
  768.6 87.1 %reduce-scatter.23.cloned.1.call-done = bf16[96,1536]{1,0:T(8,128)(2,1)} async-done(((bf16[1536,1536]{1,0:T(8,128)(2,1)}), bf16[96,1536]{1,0:T(8,128)(2,1)}) %reduce-scatter.23.cloned.1.call-update) | async-done | bytes 294928 | tf_op jit(solution)/shard_map/reduce_scatter | solution.py:302
  862.4 72.8 %reduce-scatter.9.cloned.1.call-done = bf16[96,1152]{1,0:T(8,128)(2,1)} async-done(((bf16[1536,1152]{1,0:T(8,128)(2,1)}), bf16[96,1152]{1,0:T(8,128)(2,1)}) %reduce-scatter.9.cloned.1.call-update) | async-done | bytes 221200 | tf_op jit(solution)/shard_map/reduce_scatter | solution.py:302
  935.2 85.6 %reduce-scatter.11.cloned.1.call-done = bf16[96,1536]{1,0:T(8,128)(2,1)} async-done(((bf16[1536,1536]{1,0:T(8,128)(2,1)}), bf16[96,1536]{1,0:T(8,128)(2,1)}) %reduce-scatter.11.cloned.1.call-update) | async-done | bytes 294928 | tf_op jit(solution)/shard_map/reduce_scatter | solution.py:302
  1022.6 78.1 %reduce-scatter.13.cloned.1.call-done = bf16[96,1152]{1,0:T(8,128)(2,1)} async-done(((bf16[1536,1152]{1,0:T(8,128)(2,1)}), bf16[96,1152]{1,0:T(8,128)(2,1)}) %reduce-scatter.13.cloned.1.call-update) | async-done | bytes 221200 | tf_op jit(solution)/shard_map/reduce_scatter | solution.py:302
  1100.7 86.3 %reduce-scatter.15.cloned.1.call-done = bf16[96,1536]{1,0:T(8,128)(2,1)} async-done(((bf16[1536,1536]{1,0:T(8,128)(2,1)}), bf16[96,1536]{1,0:T(8,128)(2,1)}) %reduce-scatter.15.cloned.1.call-update) | async-done | bytes 294928 | tf_op jit(solution)/shard_map/reduce_scatter | solution.py:302
  1198.1 9.3 all-to-all-done.3
  1220.8 15.4 %collective-permute-done.45 = bf16[4,24,2,2688]{3,1,2,0:T(8,128)(2,1)S(1)} collective-permute-done((bf16[4,24,2,2688]{3,1,2,0:T(8,128)(2,1)}, bf16[4,24,2,2688]{3,1,2,0:T(8,128)(2,1)S(1)}, u32[]{:S(2)}, u32[]{:S(2)}) %collective-permute-start.45) | collective-permute-done | bytes 1032224 | tf_op jit(solution)/shard_map/ppermute | solution.py:91
  (817 shorter events, 394.7 us)
Async XLA Ops:
  7.2 133.7 %all-gather.19.cloned.1.call-start = ((), (), s32[]{:S(2)}) async-start(), calls=%async_computation.21 | async-start | bytes 3760128 | tf_op jit(solution)/shard_map/all_gather | solution.py:191
  30.2 129.0 %all-gather.17.cloned.1.call-start = ((), (), s32[]{:S(2)}) async-start(), calls=%async_computation.20 | async-start | bytes 3760128 | tf_op jit(solution)/shard_map/all_gather | solution.py:191
  31.0 175.5 %all-gather.21.cloned.1.call-start = ((), (), s32[]{:S(2)}) async-start(), calls=%async_computation.22 | async-start | bytes 1253376 | tf_op jit(solution)/shard_map/all_gather | solution.py:191
  31.3 39.7 %collective-permute-start.7 = (bf16[2,120,1536]{2,1,0:T(8,128)(2,1)S(1)}, bf16[2,120,1536]{2,1,0:T(8,128)(2,1)S(1)}, u32[]{:S(2)}, u32[]{:S(2)}) collective-permute-start(bf16[2,120,1536]{2,1,0:T(8,128)(2,1)S(1)} %maximum_bitcast_fusion), channel_id=1, source_target_pairs={{0,0},{1,4},{2,8},{3,12},{4,16},{5,20},{6,24},{7,28},{8,32},{9,36}... | collective-permute-start | bytes 2211848 | tf_op jit(solution)/shard_map/ppermute | solution.py:188
  71.6 181.4 %all-gather.23.cloned.1.call-start = ((), (), s32[]{:S(2)}) async-start(), calls=%async_computation.23 | async-start | bytes 1253376 | tf_op jit(solution)/shard_map/all_gather | solution.py:191
  72.2 239.6 %all-gather.25.cloned.1.call-start = ((), (), s32[]{:S(2)}) async-start(), calls=%async_computation.24 | async-start | bytes 5013504 | tf_op jit(solution)/shard_map/all_gather | solution.py:191
  73.2 298.2 %all-gather.27.cloned.1.call-start = ((), (), s32[]{:S(2)}) async-start(), calls=%async_computation.25 | async-start | bytes 5013504 | tf_op jit(solution)/shard_map/all_gather | solution.py:191
  74.1 356.3 %all-gather.29.cloned.1.call-start = ((), (), s32[]{:S(2)}) async-start(), calls=%async_computation.26 | async-start | bytes 5013504 | tf_op jit(solution)/shard_map/all_gather | solution.py:191
  76.5 36.2 %collective-permute-start.4 = (bf16[144,1536]{1,0:T(8,128)(2,1)}, bf16[144,1536]{1,0:T(8,128)(2,1)S(1)}, u32[]{:S(2)}, u32[]{:S(2)}) collective-permute-start(bf16[144,1536]{1,0:T(8,128)(2,1)} %maximum_maximum_fusion), channel_id=1, source_target_pairs={{0,1},{1,2},{2,3},{3,0},{4,5},{5,6},{6,7},{7,4},{8,9},{9,10},{10,1... | collective-permute-start | bytes 1327112 | tf_op jit(solution)/shard_map/ppermute | solution.py:91
  78.1 36.6 %collective-permute-start.3 = (bf16[144,1536]{1,0:T(8,128)(2,1)}, bf16[144,1536]{1,0:T(8,128)(2,1)}, u32[]{:S(2)}, u32[]{:S(2)}) collective-permute-start(bf16[144,1536]{1,0:T(8,128)(2,1)} %maximum_maximum_fusion), channel_id=1, source_target_pairs={{0,3},{1,0},{2,1},{3,2},{4,7},{5,4},{6,5},{7,6},{8,11},{9,8},{10,9... | collective-permute-start | bytes 1327112 | tf_op jit(solution)/shard_map/ppermute | solution.py:91
  101.8 23.3 %all-to-all-start = ((bf16[16,2,9216]{2,1,0:T(2,128)(2,1)}), bf16[16,2,9216]{2,1,0:T(2,128)(2,1)S(1)}, u32[]{:S(2)}, u32[]{:S(2)}) async-start(bf16[16,2,9216]{2,1,0:T(2,128)(2,1)} %reshape.597), calls=%async_computation | async-start | bytes 1179648 | tf_op jit(solution)/shard_map/all_to_all | solution.py:211
  111.9 378.1 %all-gather.31.cloned.1.call-start = ((), (), s32[]{:S(2)}) async-start(), calls=%async_computation.27 | async-start | bytes 5013504 | tf_op jit(solution)/shard_map/all_gather | solution.py:191
  114.7 23.9 %collective-permute-start.5 = (bf16[72,1536]{1,0:T(8,128)(2,1)}, bf16[72,1536]{1,0:T(8,128)(2,1)}, u32[]{:S(2)}, u32[]{:S(2)}) collective-permute-start(bf16[72,1536]{1,0:T(8,128)(2,1)} %slice.698), channel_id=1, source_target_pairs={{0,1},{1,2},{2,3},{3,0},{4,5},{5,6},{6,7},{7,4},{8,9},{9,10},{10,1... | collective-permute-start | bytes 663560 | tf_op jit(solution)/shard_map/ppermute | solution.py:91
  140.4 611.5 %reduce-scatter.17.cloned.1.call-start = ((), (), s32[]{:S(2)}) async-start(), calls=%async_computation.16 | async-start | bytes 1253376 | tf_op jit(solution)/shard_map/reduce_scatter | solution.py:302
  208.6 48.8 %collective-permute-start.8 = (bf16[64,1536]{1,0:T(8,128)(2,1)S(1)}, bf16[64,1536]{1,0:T(8,128)(2,1)S(1)}, u32[]{:S(2)}, u32[]{:S(2)}) collective-permute-start(bf16[64,1536]{1,0:T(8,128)(2,1)S(1)} %slice.730), channel_id=1, source_target_pairs={{0,1},{1,2},{2,3},{3,0},{4,5},{5,6},{6,7},{7,4},{8,9},{9,10},{10,1... | collective-permute-start | bytes 589832 | tf_op jit(solution)/shard_map/ppermute | solution.py:91
  546.7 205.2 %reduce-scatter.19.cloned.1.call-start = ((), (), s32[]{:S(2)}) async-start(), calls=%async_computation.17 | async-start | bytes 5013504 | tf_op jit(solution)/shard_map/reduce_scatter | solution.py:302
  553.8 214.8 %reduce-scatter.21.cloned.1.call-start = ((), (), s32[]{:S(2)}) async-start(), calls=%async_computation.18 | async-start | bytes 1253376 | tf_op jit(solution)/shard_map/reduce_scatter | solution.py:302
  560.1 295.6 %reduce-scatter.23.cloned.1.call-start = ((), (), s32[]{:S(2)}) async-start(), calls=%async_computation.19 | async-start | bytes 5013504 | tf_op jit(solution)/shard_map/reduce_scatter | solution.py:302
  565.2 370.0 %reduce-scatter.9.cloned.1.call-start = ((), (), s32[]{:S(2)}) async-start(), calls=%async_computation.12 | async-start | bytes 3760128 | tf_op jit(solution)/shard_map/reduce_scatter | solution.py:302
  588.8 432.0 %reduce-scatter.11.cloned.1.call-start = ((), (), s32[]{:S(2)}) async-start(), calls=%async_computation.13 | async-start | bytes 5013504 | tf_op jit(solution)/shard_map/reduce_scatter | solution.py:302
  611.2 489.5 %reduce-scatter.13.cloned.1.call-start = ((), (), s32[]{:S(2)}) async-start(), calls=%async_computation.14 | async-start | bytes 3760128 | tf_op jit(solution)/shard_map/reduce_scatter | solution.py:302
  668.3 518.7 %reduce-scatter.15.cloned.1.call-start = ((), (), s32[]{:S(2)}) async-start(), calls=%async_computation.15 | async-start | bytes 5013504 | tf_op jit(solution)/shard_map/reduce_scatter | solution.py:302
  857.6 340.1 %collective-permute-start.46 = (bf16[120,2,1536]{2,0,1:T(8,128)(2,1)}, bf16[120,2,1536]{2,0,1:T(8,128)(2,1)}, u32[]{:S(2)}, u32[]{:S(2)}) collective-permute-start(bf16[120,2,1536]{2,0,1:T(8,128)(2,1)} %pad_maximum_fusion.7), channel_id=1, source_target_pairs={{0,0},{4,1},{8,2},{12,3},{16,4},{20,5},{24,6},{28,7},{32,8},{36,9}... | collective-permute-start | bytes 2211848 | tf_op jit(solution)/shard_map/ppermute | solution.py:399
  1207.5 28.7 %collective-permute-start.45 = (bf16[4,24,2,2688]{3,1,2,0:T(8,128)(2,1)}, bf16[4,24,2,2688]{3,1,2,0:T(8,128)(2,1)S(1)}, u32[]{:S(2)}, u32[]{:S(2)}) collective-permute-start(bf16[4,24,2,2688]{3,1,2,0:T(8,128)(2,1)} %all-to-all-done.3), channel_id=1, source_target_pairs={{0,64},{64,0},{1,65},{65,1},{2,66},{66,2},{3,67},{67,3},{4,68},{68... | collective-permute-start | bytes 3096584 | tf_op jit(solution)/shard_map/ppermute | solution.py:91
  (221 other events, 2945.9 us)
Sparse Core Ops, SparseCore 0:
  30.4 69.1 all-gather.18
  102.5 56.6 all-gather.16
  162.2 44.2 all-gather.20
  208.8 44.1 all-gather.22
  255.3 56.5 all-gather.24
  314.7 56.5 all-gather.26
  373.7 56.5 all-gather.28
  433.3 56.5 all-gather.30
  546.8 65.6 reduce-scatter.16
  616.9 82.5 reduce-scatter.18
  703.4 65.1 reduce-scatter.20
  773.1 82.5 reduce-scatter.22
  859.7 75.4 reduce-scatter.8
  939.1 81.5 reduce-scatter.10
  1025.2 75.4 reduce-scatter.12
  1105.2 81.7 reduce-scatter.14

commit v2 on v1

--- a/solution.py
+++ b/solution.py
@@ -5,6 +5,7 @@
 
 HEAD_DIM = 64
 SHARD = ("y", "zh", "core")
+TP = ("core", "ctx")
 OWNER = ("y", "zh", "core", "ctx")
 SLOT = ("rep", "y", "zh", "core")
 EVERY = ("rep", "y", "zh", "core", "ctx")
@@ -91,28 +92,77 @@
     return lax.ppermute(values, axis, [(i, (i + step) % count) for i in range(count)])
 
 
-def ring_gather(block):
-    half = block.shape[0] // 2 // 8 * 8
-    behind = turn(block, "ctx", 1)
-    ahead = turn(block, "ctx", -1)
-    far_top = turn(behind[:half], "ctx", 1)
-    far_bottom = turn(ahead[half:], "ctx", -1)
-    return [block, ahead, jnp.concatenate([far_top, far_bottom]), behind]
-
-
-def ring_scatter(blocks):
-    half = blocks[0].shape[0] // 2 // 8 * 8
-    from_behind = turn(blocks[2][:half], "ctx", 1)
-    from_ahead = turn(blocks[2][half:], "ctx", -1)
-    to_ahead = jnp.concatenate([blocks[1][:half] + from_behind, blocks[1][half:]])
-    to_behind = jnp.concatenate([blocks[3][:half], blocks[3][half:] + from_ahead])
-    got_behind = turn(to_ahead, "ctx", 1)
-    got_ahead = turn(to_behind, "ctx", -1)
+def cross(values):
+    return lax.ppermute(values, ("rep", "zh"), [(0, 3), (3, 0), (1, 2), (2, 1)])
+
+
+def after(values, *others):
+    return lax.optimization_barrier((values, *others))[0]
+
+
+def cut(values, axis, low, high):
+    return lax.slice_in_dim(values, low, high, axis=axis)
+
+
+def ring_gather(block, name="ctx", axis=0):
+    size = block.shape[axis]
+    half = size // 2 // 8 * 8
+    behind = turn(block, name, 1)
+    ahead = turn(block, name, -1)
+    far_top = turn(cut(behind, axis, 0, half), name, 1)
+    far_bottom = turn(cut(ahead, axis, half, size), name, -1)
+    return [block, ahead, jnp.concatenate([far_top, far_bottom], axis), behind]
+
+
+def ring_scatter(blocks, name="ctx", axis=0):
+    size = blocks[0].shape[axis]
+    half = size // 2 // 8 * 8
+    from_behind = turn(cut(blocks[2], axis, 0, half), name, 1)
+    from_ahead = turn(cut(blocks[2], axis, half, size), name, -1)
+    to_ahead = jnp.concatenate(
+        [cut(blocks[1], axis, 0, half) + from_behind, cut(blocks[1], axis, half, size)], axis
+    )
+    to_behind = jnp.concatenate(
+        [cut(blocks[3], axis, 0, half), cut(blocks[3], axis, half, size) + from_ahead], axis
+    )
+    got_behind = turn(to_ahead, name, 1)
+    got_ahead = turn(to_behind, name, -1)
     return blocks[0].astype(F32) + got_behind.astype(F32) + got_ahead.astype(F32)
 
 
 def direct_gather(block, axis):
     return [block] + [turn(block, axis, -k) for k in range(1, lax.axis_size(axis))]
+
+
+def pair(mine, axis):
+    other = cross(mine)
+    first = lax.axis_index("zh") == 0
+    return jnp.where(
+        first, jnp.concatenate([mine, other], axis), jnp.concatenate([other, mine], axis)
+    )
+
+
+def pair_sum(both_halves, axis):
+    zh = lax.axis_index("zh")
+    theirs = lax.dynamic_index_in_dim(both_halves, 1 - zh, axis, keepdims=False)
+    mine = lax.dynamic_index_in_dim(both_halves, zh, axis, keepdims=False)
+    half_sum = (mine.astype(F32) + cross(theirs).astype(F32)).astype(BF)
+    return half_sum, turn(half_sum, "rep", 1)
+
+
+def to_relative(values):
+    size = values.shape[-1]
+    return lax.dynamic_slice_in_dim(
+        jnp.concatenate([values, values], -1), lax.axis_index("y") * (size // 4), size, values.ndim - 1
+    )
+
+
+def from_relative(values):
+    size = values.shape[-1]
+    start = (4 - lax.axis_index("y")) % 4 * (size // 4)
+    return lax.dynamic_slice_in_dim(
+        jnp.concatenate([values, values], -1), start, size, values.ndim - 1
+    )
 
 
 def split_streams(blocks, image_rows, rows):
@@ -160,42 +210,25 @@
     own_rows = mod_weight.shape[0]
     span, ff = width // 4, up_weight.shape[2]
     ff_span = ff // 4
+    half_span, half_ff = span // 2, ff_span // 2
     position = lax.axis_index("ctx")
+    core = lax.axis_index("core")
     owner_index = lax.axis_index(OWNER)
     shards = 16
 
-    meta = jnp.broadcast_to(text_lengths[0, 0].astype(BF), (8, width))
-    token_blocks = ring_gather(jnp.concatenate([image_tokens[0], text_tokens[0], meta]))
-    image_all, text_all = split_streams(token_blocks, image_rows, rows)
-    lengths = [b[rows, 0].astype(F32) for b in token_blocks]
-    cotan_blocks = ring_gather(jnp.concatenate([image_cotan[0], text_cotan[0]]))
-    image_cot_all, text_cot_all = split_streams(cotan_blocks, image_rows, rows)
-
-    col_send = jnp.concatenate(
-        [
-            qkv_weight.reshape(own_rows, 2, 3, 4, span)
-            .transpose(3, 1, 0, 2, 4)
-            .reshape(4, 2, own_rows, 3 * span),
-            up_weight.reshape(own_rows, 2, 4, ff_span).transpose(2, 1, 0, 3),
-        ],
-        axis=3,
-    )
-    col_got = lax.all_to_all(col_send, "ctx", split_axis=0, concat_axis=0, tiled=True)
-    col_got = col_got.transpose(1, 0, 2, 3).reshape(2, 4 * own_rows, -1)
-    to_slice = [(b, (b % shards) * 4 + b // shards) for b in range(4 * shards)]
-    from_slice = [(d, s) for s, d in to_slice]
-    row_send = jnp.concatenate([out_weight, down_weight]).transpose(1, 0, 2)
-    row_got = lax.ppermute(row_send, OWNER, to_slice)
-
-    def gather_rows(values):
-        return lax.all_gather(values, SHARD, axis=0, tiled=True)
-
-    qkv_cols = [gather_rows(col_got[t, :, : 3 * span]) for t in range(2)]
-    out_rows = [gather_rows(row_got[t, :own_rows]) for t in range(2)]
-    up_cols = [gather_rows(col_got[t, :, 3 * span :]) for t in range(2)]
-    down_rows = [gather_rows(row_got[t, own_rows:]) for t in range(2)]
-
-    all_sequences = lax.all_gather(slot_sequence, SLOT, axis=0, tiled=True)
+    def from_columns(columns):
+        got = lax.all_to_all(columns, TP, split_axis=0, concat_axis=0, tiled=True)
+        return got.transpose(1, 0, 2, 3).reshape(2, 8 * own_rows, -1)
+
+    qkv_got = from_columns(
+        qkv_weight.reshape(own_rows, 2, 3, 4, 2, half_span)
+        .transpose(4, 3, 1, 0, 2, 5)
+        .reshape(8, 2, own_rows, 3 * half_span)
+    )
+    qkv_own = jnp.concatenate(ring_gather(pair(qkv_got, 1), "y", 1), 1)
+    qkv_cols = (qkv_own, turn(qkv_own, "core", 1))
+
+    all_sequences = lax.all_gather(after(slot_sequence, qkv_got), SLOT, axis=0, tiled=True)
     slot_hot = (
         all_sequences[:, None] == jnp.arange(seq_total, dtype=jnp.int32)[None, :]
     ).astype(F32)
@@ -216,6 +249,35 @@
         + mod_bias.astype(F32).reshape(2, 6, width)
     ) * live
 
+    meta = jnp.broadcast_to(text_lengths[0, 0].astype(BF), (8, width))
+    own_tokens = jnp.concatenate([image_tokens[0], text_tokens[0], meta])
+    token_blocks = ring_gather(to_relative(after(own_tokens, qkv_got)))
+    image_all, text_all = split_streams(token_blocks, image_rows, rows)
+    lengths = [b[rows, 0].astype(F32) for b in token_blocks]
+    own_cots = jnp.concatenate([image_cotan[0], text_cotan[0]])
+    cotan_blocks = ring_gather(after(own_cots, got_mod))
+    image_cot_all, text_cot_all = split_streams(cotan_blocks, image_rows, rows)
+
+    to_slice = []
+    for source in range(4 * shards):
+        y, zh, k, c = source // 16, source // 8 % 2, source // 4 % 2, source % 4
+        to_slice.append((source, ((c * 2 + k) * 2 + zh) * 4 + y))
+    from_slice = [(d, s) for s, d in to_slice]
+    out_got = lax.ppermute(after(out_weight, got_mod).transpose(1, 0, 2), OWNER, to_slice)
+    out_own = pair(lax.all_gather(out_got, "y", axis=1, tiled=True), 1)
+    out_rows = jnp.concatenate([out_own, turn(out_own, "core", 1)], 1)
+    up_got = from_columns(
+        after(up_weight, got_mod)
+        .reshape(own_rows, 2, 4, 2, half_ff)
+        .transpose(3, 2, 1, 0, 4)
+        .reshape(8, 2, own_rows, half_ff)
+    )
+    up_own = jnp.concatenate(ring_gather(pair(up_got, 1), "y", 1), 1)
+    up_cols = (up_own, turn(up_own, "core", 1))
+    down_got = lax.ppermute(after(down_weight, got_mod).transpose(1, 0, 2), OWNER, to_slice)
+    down_own = pair(lax.all_gather(down_got, "y", axis=1, tiled=True), 1)
+    down_rows = (down_own, turn(down_own, "core", 1))
+
     own_masks = (
         jnp.full((image_rows, 1), 1.0, F32) * live,
         (jnp.arange(text_cap, dtype=jnp.int32) < text_lengths[0, 0]).astype(F32)[:, None] * live,
@@ -227,21 +289,33 @@
     key_bias = jnp.concatenate(
         [jnp.zeros((4 * image_rows,), F32), (text_valid - 1.0) * 1000000000.0]
     )
-    bias_at = lambda values, start, size: lax.dynamic_slice_in_dim(values, start, size, 1)
-    q_bias = bias_at(qv_bias, position * span, span).astype(F32)
-    v_bias = bias_at(qv_bias, width + position * span, span).astype(F32)
-    up_part = bias_at(up_bias, position * ff_span, ff_span).astype(F32)
-    normed_first, modulated_first, queries, keys, values = ([], [], [], [], [])
+
+    def bias_part(values, start, size):
+        return [
+            lax.dynamic_slice_in_dim(values, start + k * size, size, 1).astype(F32)
+            for k in (core, 1 - core)
+        ]
+
+    q_bias = bias_part(qv_bias, position * span, half_span)
+    v_bias = bias_part(qv_bias, width + position * span, half_span)
+    up_part = bias_part(up_bias, position * ff_span, half_ff)
+    first_mod = to_relative(modulation[:, :2])
+    normed_first, modulated_first = ([], [])
+    parts = [[], [], []]
     for t, tokens in enumerate((image_all, text_all)):
         normed, _ = norm_rows(tokens.astype(F32))
-        modulated = (normed * (1.0 + modulation[t, 1]) + modulation[t, 0]).astype(BF)
-        projected = mm(modulated, qkv_cols[t])
-        queries.append((projected[:, :span] + q_bias[t]).astype(BF))
-        keys.append(projected[:, span : 2 * span].astype(BF))
-        values.append((projected[:, 2 * span :] + v_bias[t]).astype(BF))
+        modulated = (normed * (1.0 + first_mod[t, 1]) + first_mod[t, 0]).astype(BF)
+        pieces = [[], [], []]
+        for h in range(2):
+            projected = mm(modulated, qkv_cols[h][t])
+            pieces[0].append((projected[:, :half_span] + q_bias[h][t]).astype(BF))
+            pieces[1].append(projected[:, half_span : 2 * half_span].astype(BF))
+            pieces[2].append((projected[:, 2 * half_span :] + v_bias[h][t]).astype(BF))
+        for part, piece in zip(parts, pieces):
+            part.append(jnp.concatenate(piece, 1))
         normed_first.append(normed)
         modulated_first.append(modulated)
-    query, all_keys, all_values = (jnp.concatenate(v) for v in (queries, keys, values))
+    query, all_keys, all_values = (jnp.concatenate(v) for v in parts)
     mixed, log_total = attention_forward(query, all_keys, all_values, key_bias)
     count = 4 * image_rows
     mixed_parts = (mixed[:count], mixed[count:])
@@ -275,21 +349,29 @@
     normed_two, inv_two = norm_rows(middle)
     modulated_two = (normed_two * both(4, 1.0) + both(3)).astype(BF)
 
-    seconds = split_streams(ring_gather(modulated_two), image_rows, rows)
+    seconds = split_streams(ring_gather(to_relative(modulated_two)), image_rows, rows)
     branch_grads = (
         (image_cot_all.astype(F32) * live * modulation[0, 5]).astype(BF),
         (text_cot_all.astype(F32) * (text_valid * live)[:, None] * modulation[1, 5]).astype(BF),
     )
     actives, hidden_grads, down_parts, second_parts = ([], [], [], [])
     for t in range(2):
-        hidden = mm(seconds[t], up_cols[t]) + up_part[t]
-        activated, pull = jax.vjp(gelu_tanh, hidden)
-        actives.append(activated.astype(BF))
-        grad_active = mm_nt(branch_grads[t], down_rows[t])
-        hidden_grads.append(pull(grad_active)[0].astype(BF))
-        second_parts.append(mm_nt(hidden_grads[t], up_cols[t]).astype(BF))
-        down_parts.append(mm(actives[t], down_rows[t]).astype(BF))
-    grad_two = ring_scatter(join_streams(*second_parts))
+        active_halves, grad_halves = ([], [])
+        for h in range(2):
+            hidden = mm(seconds[t], up_cols[h][t]) + up_part[h][t]
+            activated, pull = jax.vjp(gelu_tanh, hidden)
+            active_halves.append(activated.astype(BF))
+            grad_active = mm_nt(branch_grads[t], down_rows[h][t])
+            grad_halves.append(pull(grad_active)[0].astype(BF))
+        second_parts.append(
+            (mm_nt(grad_halves[0], up_cols[0][t]) + mm_nt(grad_halves[1], up_cols[1][t])).astype(BF)
+        )
+        down_parts.append(
+            (mm(active_halves[0], down_rows[0][t]) + mm(active_halves[1], down_rows[1][t])).astype(BF)
+        )
+        actives.append(active_halves)
+        hidden_grads.append(grad_halves)
+    grad_two = from_relative(ring_scatter(join_streams(*second_parts)))
     grad_middle = own_cotan + norm_back(grad_two * both(4, 1.0), normed_two, inv_two)
     grad_attn = (grad_middle * both(2)).astype(BF)
     attn_grads = split_streams(ring_gather(grad_attn), image_rows, rows)
@@ -298,28 +380,72 @@
     outs = ((middle + both(5) * branch) * row_mask).astype(BF)
     grad_gate_two = sums(own_cotan * branch)
 
-    def scatter_rows(values):
-        return lax.psum_scatter(values, SHARD, scatter_dimension=0, tiled=True)
-
-    down_own = [scatter_rows(mm_tn(actives[t], branch_grads[t]).astype(BF)) for t in range(2)]
-    up_own = [scatter_rows(mm_tn(seconds[t], hidden_grads[t]).astype(BF)) for t in range(2)]
+    def core_sum(own, other):
+        return (own.astype(F32) + turn(other, "core", 1).astype(F32)).astype(BF)
+
+    def columns_total(lefts, rights):
+        own, other = (
+            jnp.stack([mm_tn(lefts[t], rights[t][h]).astype(BF) for t in range(2)]) for h in range(2)
+        )
+        summed = core_sum(own, other)
+        quarter = summed.shape[1] // 4
+        blocks = [cut(summed, 1, j * quarter, (j + 1) * quarter) for j in range(4)]
+        mine = ring_scatter(blocks, "y", 1).astype(BF)
+        total, more = pair_sum(mine.reshape(2, 2, quarter // 2, -1), 1)
+        total = (total.astype(F32) + more.astype(F32)).astype(BF)
+        total = total.reshape(2, 8, own_rows, -1).transpose(1, 0, 2, 3)
+        total = lax.all_to_all(total, TP, split_axis=0, concat_axis=0, tiled=True)
+        return total.reshape((2, 4) + total.shape[1:]).astype(F32)
+
+    def rows_total(lefts, rights):
+        own, other = (
+            jnp.stack([mm_tn(lefts[t][h], rights[t]).astype(BF) for t in range(2)]) for h in range(2)
+        )
+        summed = core_sum(own, other)
+        summed = summed.reshape(4, summed.shape[1] // 2, -1)
+        mine = lax.psum_scatter(summed, "y", scatter_dimension=1, tiled=True)
+        total, more = pair_sum(mine.reshape((2, 2) + mine.shape[1:]), 1)
+        total = (total.astype(F32) + more.astype(F32)).astype(BF)
+        return lax.ppermute(total, OWNER, from_slice).astype(F32).transpose(1, 0, 2)
+
+    down_grad = rows_total(actives, branch_grads)
+    up_total = columns_total(seconds, hidden_grads)
+    up_grad = up_total.transpose(3, 2, 1, 0, 4).reshape(up_weight.shape)
 
     grad_mixed = jnp.concatenate([mm_nt(attn_grads[t], out_rows[t]).astype(BF) for t in range(2)])
-    out_own = [scatter_rows(mm_tn(mixed_parts[t], attn_grads[t]).astype(BF)) for t in range(2)]
+    out_grad = rows_total([(m[:, :half_span], m[:, half_span:]) for m in mixed_parts], attn_grads)
     grad_qkv = attention_backward(query, all_keys, all_values, key_bias, log_total, grad_mixed)
-    grad_qkv = jnp.concatenate(grad_qkv, axis=1)
-    proj_grads = (grad_qkv[:count], grad_qkv[count:])
-    first_parts = [mm_nt(proj_grads[t], qkv_cols[t]) for t in range(2)]
-    grad_one = ring_scatter(join_streams(*(f.astype(BF) for f in first_parts)))
-    qkv_own = [scatter_rows(mm_tn(modulated_first[t], proj_grads[t]).astype(BF)) for t in range(2)]
+    proj_grads = []
+    for low, high in ((0, count), (count, 4 * rows)):
+        proj_grads.append(
+            [
+                jnp.concatenate(
+                    [g[low:high, h * half_span : (h + 1) * half_span] for g in grad_qkv], axis=1
+                )
+                for h in range(2)
+            ]
+        )
+    first_parts = [
+        mm_nt(proj_grads[t][0], qkv_cols[0][t]) + mm_nt(proj_grads[t][1], qkv_cols[1][t])
+        for t in range(2)
+    ]
+    grad_one = from_relative(ring_scatter(join_streams(*(f.astype(BF) for f in first_parts))))
+    qkv_total = columns_total(modulated_first, proj_grads)
+    qkv_grad = (
+        qkv_total.reshape(2, 4, 2, own_rows, 3, half_span)
+        .transpose(3, 2, 4, 1, 0, 5)
+        .reshape(qkv_weight.shape)
+    )
 
     normed_one, inv_one = norm_rows(tokens)
     input_grad = grad_middle + norm_back(grad_one * both(1, 1.0), normed_one, inv_one)
 
     vectors = jnp.stack(
         [
-            jnp.stack([jnp.sum(f, 0) for f in first_parts]),
-            jnp.stack([jnp.sum(f * n, 0) for f, n in zip(first_parts, normed_first)]),
+            from_relative(jnp.stack([jnp.sum(f, 0) for f in first_parts])),
+            from_relative(
+                jnp.stack([jnp.sum(f * n, 0) for f, n in zip(first_parts, normed_first)])
+            ),
             sums(grad_middle * attn),
             sums(grad_two),
             sums(grad_two * normed_two),
@@ -333,10 +459,21 @@
     vectors = jnp.sum(
         lax.all_to_all(vectors, "ctx", split_axis=0, concat_axis=0, tiled=True), axis=0
     )
-    qv_sums = jnp.stack([jnp.sum(g.astype(F32), 0) for g in proj_grads]).reshape(2, 3, span)
-    up_sums = jnp.stack([jnp.sum(g.astype(F32), 0) for g in hidden_grads])
+    def in_order(halves):
+        mine, other = (jnp.sum(h.astype(F32), 0) for h in halves)
+        return jnp.where(
+            core == 0, jnp.concatenate([mine, other], -1), jnp.concatenate([other, mine], -1)
+        )
+
+    q_sums, v_sums = (
+        jnp.stack(
+            [in_order([h[:, a * half_span : (a + 1) * half_span] for h in g]) for g in proj_grads]
+        )
+        for a in (0, 2)
+    )
+    up_sums = jnp.stack([in_order(g) for g in hidden_grads])
     own_vector = jnp.concatenate(
-        [vectors, qv_sums[:, 0].reshape(-1), qv_sums[:, 2].reshape(-1), up_sums.reshape(-1)]
+        [vectors, q_sums.reshape(-1), v_sums.reshape(-1), up_sums.reshape(-1)]
     ).astype(BF)
     size = own_vector.shape[0]
     gathered = own_vector.reshape(1, 1, 1, 1, 4, size // 4)
@@ -372,12 +509,12 @@
     out_bias_grad = owner_slice(jnp.sum(table[:, :, 6].astype(F32), 0))
     down_bias_grad = owner_slice(jnp.sum(table[:, :, 7].astype(F32), 0))
     rest = jnp.sum(everything[:, :, vec_size:].astype(F32), 0)
-    q_total, v_total, up_total = (
+    q_total, v_total, u_total = (
         rest[:, a:b].reshape(4, 2, -1).transpose(1, 0, 2).reshape(2, -1)
         for a, b in ((0, 2 * span), (2 * span, 4 * span), (4 * span, 4 * span + 2 * ff_span))
     )
     qv_bias_grad = owner_slice(jnp.concatenate([q_total, v_total], axis=1))
-    up_bias_grad = owner_slice(up_total)
+    up_bias_grad = owner_slice(u_total)
     slot_grads = mm_nt(mod_rows, mod_matrix)
     grad_cond_cols = lax.dot_general(
         slot_hot, slot_grads, (((0,), (0,)), ((), ())), precision=lax.Precision.HIGHEST
@@ -385,28 +522,6 @@
     cond_part = lax.dynamic_slice_in_dim(cond_float, owner_index * own_rows, own_rows, 1)
     cond_grad = jax.vjp(jax.nn.silu, cond_part)[1](grad_cond_cols)[0]
 
-    col_back = jnp.stack(
-        [
-            jnp.concatenate([qkv_own[t], up_own[t]], axis=1).reshape(4, own_rows, -1)
-            for t in range(2)
-        ],
-        axis=2,
-    )
-    col_back = lax.all_to_all(col_back, "ctx", split_axis=0, concat_axis=0, tiled=True)
-    row_back = jnp.stack(
-        [jnp.concatenate([out_own[t], down_own[t]]) for t in range(2)], axis=1
-    )
-    row_back = lax.ppermute(row_back, OWNER, from_slice)
-    col_back = col_back.astype(F32) + turn(col_back, "rep", 1).astype(F32)
-    row_back = row_back.astype(F32) + turn(row_back, "rep", 1).astype(F32)
-    qkv_grad = (
-        col_back[..., : 3 * span]
-        .reshape(4, own_rows, 2, 3, span)
-        .transpose(1, 2, 3, 0, 4)
-        .reshape(qkv_weight.shape)
-    )
-    up_grad = col_back[..., 3 * span :].transpose(1, 2, 0, 3).reshape(up_weight.shape)
-    out_grad, down_grad = (row_back[:own_rows], row_back[own_rows:])
     return (
         outs[None, :image_rows],
         outs[None, image_rows:],

time: 1260 us -> 863 us (0.68)
  the two profiles are of different devices: /device:TPU:1 before, /device:TPU:7 now
where the time goes in v2:
time: 863 us; the launch traced here: 854 us
  waiting for transfers between devices  219 us (25%)
  starting transfers between devices  172 us (20%)
  local copies, waits for them, and re-layouts  169 us (20%)
  other arithmetic  126 us (15%)
  matrix products  112 us (13%)
  blocking collectives  33.5 us (4%)
  between operations  21.9 us (3%)
    ppermute x72, waiting for transfers between devices, turn(): lax.ppermute(values, axis, [(i, (i + step) % count) for i in range(count)])  132 us
    ppermute x72, starting transfers between devices, turn(): lax.ppermute(values, axis, [(i, (i + step) % count) for i in range(count)])  94.2 us
    ppermute x8, waiting for transfers between devices, cross(): return lax.ppermute(values, ('rep', 'zh'), [(0, 3), (3, 0), (1, 2), (2, 1)])  55 us
    unnamed x486, local copies, waits for them, and re-layouts  50.5 us
    dot_general x17, matrix products, mm_tn(): lax.dot_general(left, right, (((0,), (0,)), ((), ())), preferred_element_...  35.5 us
    dot_general x15, matrix products, mm_nt(): lax.dot_general(left, right, (((1,), (1,)), ((), ())), preferred_element_...  33 us
    dot_general x16, matrix products, mm(): return jnp.dot(left, right, preferred_element_type=F32)  26.5 us
    all_gather x1, blocking collectives, per_device(): out_own = pair(lax.all_gather(out_got, 'y', axis=1, tiled=True), 1)  19.1 us
  transfers between devices with their start and end apart: 93, of which 32 were waited for; matrix products, arithmetic and copies ran while one was open for 45% of the time, Pallas kernels for 0%

profile of v2, /device:TPU:7, one launch (start us, length us, event | category | flops | bytes accessed | tf_op | source)
XLA Modules:
  0.0 854.1 jit_solution(7058950326886312936)
XLA Ops:
  19.9 14.4 %all-reduce.2 = s32[32]{0:T(128)S(1)} all-reduce(s32[32]{0:T(128)S(1)} %dynamic-update-slice), channel_id=1, replica_groups=mesh['rep'=2,'y'=4,'zh'=2,'core'=2,'ctx'=4] {'rep','y','zh','core'}, use_global_device_ids=true, to_apply=%add.2 | all-reduce | flops 32 | bytes 256
  44.1 7.9 all-to-all-start.1
  72.5 9.0 %all-to-all-start.2 = ((bf16[8,2,24,768]{3,2,1,0:T(8,128)(2,1)}), bf16[8,2,24,768]{3,2,1,0:T(8,128)(2,1)}, u32[]{:S(2)}, u32[]{:S(2)}) async-start(bf16[8,2,24,768]{3,2,1,0:T(8,128)(2,1)} %bitcast.36), calls=%async_computation.2 | async-start | bytes 1179648 | tf_op jit(solution)/shard_map/all_to_all | solution.py:220
  95.7 9.6 %collective-permute-done.13 = bf16[2,24,1536]{2,1,0:T(8,128)(2,1)} collective-permute-done((bf16[2,24,1536]{2,1,0:T(8,128)(2,1)}, bf16[2,24,1536]{2,1,0:T(8,128)(2,1)}, u32[]{:S(2)}, u32[]{:S(2)}) %collective-permute-start.13) | collective-permute-done | bytes 147488 | tf_op jit(solution)/shard_map/ppermute | solution.py:266
  105.4 19.1 %all_gather.10 = bf16[2,96,1536]{2,1,0:T(8,128)(2,1)} all-gather(bf16[2,24,1536]{2,1,0:T(8,128)(2,1)} %collective-permute-done.13), channel_id=1, replica_groups=mesh['rep'=2,'y'=4,'zh'=2,'core'=2,'ctx'=4] {'y'}, dimensions={1}, use_global_device_ids=true | all-gather | bytes 737280 | tf_op jit(solution)/shard_map/all_gather | solution.py:267
  134.3 8.5 collective-permute-start.29
  153.8 19.2 %collective-permute-done.10 = bf16[2,192,576]{2,1,0:T(8,128)(2,1)} collective-permute-done((bf16[2,192,576]{2,1,0:T(8,128)(2,1)}, bf16[2,192,576]{2,1,0:T(8,128)(2,1)}, u32[]{:S(2)}, u32[]{:S(2)}) %collective-permute-start.10) | collective-permute-done | bytes 442400 | tf_op jit(solution)/shard_map/ppermute | solution.py:92
  173.0 6.3 collective-permute-start.5
  183.1 6.3 copy.303
  197.3 13.8 %collective-permute-done.24 = bf16[2,192,768]{2,1,0:T(8,128)(2,1)} collective-permute-done((bf16[2,192,768]{2,1,0:T(8,128)(2,1)}, bf16[2,192,768]{2,1,0:T(8,128)(2,1)}, u32[]{:S(2)}, u32[]{:S(2)}) %collective-permute-start.24) | collective-permute-done | bytes 589856 | tf_op jit(solution)/shard_map/ppermute | solution.py:96
  227.6 25.4 %collective-permute-done.26 = bf16[2,384,768]{2,1,0:T(8,128)(2,1)} collective-permute-done((bf16[2,384,768]{2,1,0:T(8,128)(2,1)}, bf16[2,384,768]{2,1,0:T(8,128)(2,1)}, u32[]{:S(2)}, u32[]{:S(2)}) %collective-permute-start.26) | collective-permute-done | bytes 1179680 | tf_op jit(solution)/shard_map/ppermute | solution.py:92
  256.8 13.9 %collective-permute-start.28 = (bf16[2,192,768]{2,1,0:T(8,128)(2,1)}, bf16[2,192,768]{2,1,0:T(8,128)(2,1)}, u32[]{:S(2)}, u32[]{:S(2)}) collective-permute-start(bf16[2,192,768]{2,1,0:T(8,128)(2,1)} %slice.1011), channel_id=1, source_target_pairs={{0,48},{16,0},{32,16},{48,32},{1,49},{17,1},{33,17},{49,33},{2,50}... | collective-permute-start | bytes 1769480 | tf_op jit(solution)/shard_map/ppermute | solution.py:92
  341.9 24.4 %collective-permute-done.30 = bf16[2,384,1536]{2,1,0:T(8,128)(2,1)S(1)} collective-permute-done((bf16[2,384,1536]{2,1,0:T(8,128)(2,1)}, bf16[2,384,1536]{2,1,0:T(8,128)(2,1)S(1)}, u32[]{:S(2)}, u32[]{:S(2)}) %collective-permute-start.30) | collective-permute-done | bytes 2359328 | tf_op jit(solution)/shard_map/ppermute | solution.py:96
  444.6 15.2 %collective-permute-done.42 = bf16[136,1536]{1,0:T(8,128)(2,1)S(1)} collective-permute-done((bf16[136,1536]{1,0:T(8,128)(2,1)S(1)}, bf16[136,1536]{1,0:T(8,128)(2,1)S(1)}, u32[]{:S(2)}, u32[]{:S(2)}) %collective-permute-start.42) | collective-permute-done | bytes 417824 | tf_op jit(solution)/shard_map/ppermute | solution.py:92
  594.5 7.2 add_convert_fusion
  620.6 7.1 collective-permute-start.61
  675.0 10.8 %collective-permute-done.63 = bf16[2,192,576]{2,1,0:T(8,128)(2,1)} collective-permute-done((bf16[2,192,576]{2,1,0:T(8,128)(2,1)}, bf16[2,192,576]{2,1,0:T(8,128)(2,1)}, u32[]{:S(2)}, u32[]{:S(2)}) %collective-permute-start.63) | collective-permute-done | bytes 442400 | tf_op jit(solution)/shard_map/ppermute | solution.py:92
  730.0 6.9 collective-permute-done.66
  752.4 9.8 %collective-permute-done.77 = bf16[2,384,768]{2,1,0:T(8,128)(2,1)} collective-permute-done((bf16[2,384,768]{2,1,0:T(8,128)(2,1)}, bf16[2,384,768]{2,1,0:T(8,128)(2,1)}, u32[]{:S(2)}, u32[]{:S(2)}) %collective-permute-start.77) | collective-permute-done | bytes 1179680 | tf_op jit(solution)/shard_map/ppermute | solution.py:92
  772.2 6.7 all-to-all-start.4
  781.9 10.8 %collective-permute-done.81 = bf16[2,96,1536]{2,1,0:T(8,128)(2,1)} collective-permute-done((bf16[2,96,1536]{2,1,0:T(8,128)(2,1)}, bf16[2,96,1536]{2,1,0:T(8,128)(2,1)}, u32[]{:S(2)}, u32[]{:S(2)}) %collective-permute-start.81) | collective-permute-done | bytes 589856 | tf_op jit(solution)/shard_map/ppermute | solution.py:96
  794.0 9.7 %collective-permute-start.72 = (bf16[2,24,1536]{2,1,0:T(8,128)(2,1)S(1)}, bf16[2,24,1536]{2,1,0:T(8,128)(2,1)S(1)}, u32[]{:S(2)}, u32[]{:S(2)}) collective-permute-start(bf16[2,24,1536]{2,1,0:T(8,128)(2,1)S(1)} %add_convert_fusion.10), channel_id=1, source_target_pairs={{0,0},{16,1},{32,2},{48,3},{8,4},{24,5},{40,6},{56,7},{4,8},{20,9}... | collective-permute-start | bytes 442376 | tf_op jit(solution)/shard_map/ppermute | solution.py:409
  810.0 7.6 collective-permute-start.83
  826.0 18.3 %collective-permute-done.83 = bf16[2,96,1536]{2,1,0:T(8,128)(2,1)} collective-permute-done((bf16[2,96,1536]{2,1,0:T(8,128)(2,1)}, bf16[2,96,1536]{2,1,0:T(8,128)(2,1)}, u32[]{:S(2)}, u32[]{:S(2)}) %collective-permute-start.83) | collective-permute-done | bytes 589856 | tf_op jit(solution)/shard_map/ppermute | solution.py:409
  (1053 shorter events, 544.4 us)
Async XLA Ops:
  57.6 67.4 %collective-permute-start.4 = (bf16[144,1536]{1,0:T(8,128)(2,1)}, bf16[144,1536]{1,0:T(8,128)(2,1)}, u32[]{:S(2)}, u32[]{:S(2)}) collective-permute-start(bf16[144,1536]{1,0:T(8,128)(2,1)} %fusion.149), channel_id=1, source_target_pairs={{0,1},{1,2},{2,3},{3,0},{4,5},{5,6},{6,7},{7,4},{8,9},{9,10},{10,1... | collective-permute-start | bytes 1327112 | tf_op jit(solution)/shard_map/ppermute | solution.py:92
  72.5 120.1 %all-to-all-start.2 = ((bf16[8,2,24,768]{3,2,1,0:T(8,128)(2,1)}), bf16[8,2,24,768]{3,2,1,0:T(8,128)(2,1)}, u32[]{:S(2)}, u32[]{:S(2)}) async-start(bf16[8,2,24,768]{3,2,1,0:T(8,128)(2,1)} %bitcast.36), calls=%async_computation.2 | async-start | bytes 1179648 | tf_op jit(solution)/shard_map/all_to_all | solution.py:220
  81.6 230.4 %all-gather.2.cloned.1.call-start = ((), (), s32[]{:S(2)}) async-start(), calls=%async_computation.8 | async-start | bytes 2949120 | tf_op jit(solution)/shard_map/all_gather | solution.py:278
  82.2 42.2 %collective-permute-start.3 = (bf16[144,1536]{1,0:T(8,128)(2,1)}, bf16[144,1536]{1,0:T(8,128)(2,1)S(1)}, u32[]{:S(2)}, u32[]{:S(2)}) collective-permute-start(bf16[144,1536]{1,0:T(8,128)(2,1)} %fusion.149), channel_id=1, source_target_pairs={{0,3},{1,0},{2,1},{3,2},{4,7},{5,4},{6,5},{7,6},{8,11},{9,8},{10,9... | collective-permute-start | bytes 1327112 | tf_op jit(solution)/shard_map/ppermute | solution.py:92
  92.0 53.3 %collective-permute-start.9 = (bf16[2,384,576]{1,2,0:T(8,128)(2,1)}, bf16[2,384,576]{1,2,0:T(8,128)(2,1)}, u32[]{:S(2)}, u32[]{:S(2)}) collective-permute-start(bf16[2,384,576]{1,2,0:T(8,128)(2,1)} %copy.297), channel_id=1, source_target_pairs={{0,16},{16,32},{32,48},{48,0},{1,17},{17,33},{33,49},{49,1},{2,18}... | collective-permute-start | bytes 2654216 | tf_op jit(solution)/shard_map/ppermute | solution.py:92
  92.1 57.0 %collective-permute-start.8 = (bf16[2,384,576]{1,2,0:T(8,128)(2,1)}, bf16[2,384,576]{1,2,0:T(8,128)(2,1)}, u32[]{:S(2)}, u32[]{:S(2)}) collective-permute-start(bf16[2,384,576]{1,2,0:T(8,128)(2,1)} %copy.297), channel_id=1, source_target_pairs={{0,48},{16,0},{32,16},{48,32},{1,49},{17,1},{33,17},{49,33},{2,50}... | collective-permute-start | bytes 2654216 | tf_op jit(solution)/shard_map/ppermute | solution.py:92
  124.5 196.0 %collective-permute-start.38 = (bf16[136,1536]{1,0:T(8,128)(2,1)}, bf16[136,1536]{1,0:T(8,128)(2,1)}, u32[]{:S(2)}, u32[]{:S(2)}) collective-permute-start(bf16[136,1536]{1,0:T(8,128)(2,1)} %pad_maximum_fusion.22), channel_id=1, source_target_pairs={{0,1},{1,2},{2,3},{3,0},{4,5},{5,6},{6,7},{7,4},{8,9},{9,10},{10,1... | collective-permute-start | bytes 1253384 | tf_op jit(solution)/shard_map/ppermute | solution.py:92
  134.3 60.7 %collective-permute-start.29 = (bf16[2,96,1536]{2,1,0:T(8,128)(2,1)}, bf16[2,96,1536]{2,1,0:T(8,128)(2,1)}, u32[]{:S(2)}, u32[]{:S(2)}) collective-permute-start(bf16[2,96,1536]{2,1,0:T(8,128)(2,1)} %bitcast.315), channel_id=1, source_target_pairs={{0,0},{1,16},{2,32},{3,48},{4,8},{5,24},{6,40},{7,56},{8,4},{9,20}... | collective-permute-start | bytes 1769480 | tf_op jit(solution)/shard_map/ppermute | solution.py:277
  143.5 51.6 %collective-permute-start.14 = (bf16[2,96,1536]{2,1,0:T(8,128)(2,1)}, bf16[2,96,1536]{2,1,0:T(8,128)(2,1)}, u32[]{:S(2)}, u32[]{:S(2)}) collective-permute-start(bf16[2,96,1536]{2,1,0:T(8,128)(2,1)} %all_gather.10), channel_id=1, source_target_pairs={{0,72},{72,0},{8,64},{64,8},{1,73},{73,1},{9,65},{65,9},{2,74},{74... | collective-permute-start | bytes 1769480 | tf_op jit(solution)/shard_map/ppermute | solution.py:96
  189.4 81.3 %collective-permute-start.12 = (bf16[2,1536,576]{1,2,0:T(8,128)(2,1)}, bf16[2,1536,576]{1,2,0:T(8,128)(2,1)}, u32[]{:S(2)}, u32[]{:S(2)}) collective-permute-start(bf16[2,1536,576]{1,2,0:T(8,128)(2,1)} %copy.303), channel_id=1, source_target_pairs={{0,4},{4,0},{1,5},{5,1},{2,6},{6,2},{3,7},{7,3},{8,12},{12,8},{9,1... | collective-permute-start | bytes 10616840 | tf_op jit(solution)/shard_map/ppermute | solution.py:92
  197.2 91.7 %collective-permute-start.15 = (bf16[2,192,1536]{2,1,0:T(8,128)(2,1)S(1)}, bf16[2,192,1536]{2,1,0:T(8,128)(2,1)}, u32[]{:S(2)}, u32[]{:S(2)}) collective-permute-start(bf16[2,192,1536]{2,1,0:T(8,128)(2,1)S(1)} %maximum_select_fusion.3), channel_id=1, source_target_pairs={{0,4},{4,0},{1,5},{5,1},{2,6},{6,2},{3,7},{7,3},{8,12},{12,8},{9,1... | collective-permute-start | bytes 3538952 | tf_op jit(solution)/shard_map/ppermute | solution.py:92
  214.4 40.5 %collective-permute-start.25 = (bf16[2,384,768]{2,1,0:T(8,128)(2,1)}, bf16[2,384,768]{2,1,0:T(8,128)(2,1)}, u32[]{:S(2)}, u32[]{:S(2)}) collective-permute-start(bf16[2,384,768]{2,1,0:T(8,128)(2,1)} %get-tuple-element.202), channel_id=1, source_target_pairs={{0,48},{16,0},{32,16},{48,32},{1,49},{17,1},{33,17},{49,33},{2,50}... | collective-permute-start | bytes 3538952 | tf_op jit(solution)/shard_map/ppermute | solution.py:92
  214.4 38.6 %collective-permute-start.26 = (bf16[2,384,768]{2,1,0:T(8,128)(2,1)}, bf16[2,384,768]{2,1,0:T(8,128)(2,1)}, u32[]{:S(2)}, u32[]{:S(2)}) collective-permute-start(bf16[2,384,768]{2,1,0:T(8,128)(2,1)} %get-tuple-element.202), channel_id=1, source_target_pairs={{0,16},{16,32},{32,48},{48,0},{1,17},{17,33},{33,49},{49,1},{2,18}... | collective-permute-start | bytes 3538952 | tf_op jit(solution)/shard_map/ppermute | solution.py:92
  254.9 47.2 %collective-permute-start.27 = (bf16[2,192,768]{2,1,0:T(8,128)(2,1)}, bf16[2,192,768]{2,1,0:T(8,128)(2,1)}, u32[]{:S(2)}, u32[]{:S(2)}) collective-permute-start(bf16[2,192,768]{2,1,0:T(8,128)(2,1)} %slice.1010), channel_id=1, source_target_pairs={{0,16},{16,32},{32,48},{48,0},{1,17},{17,33},{33,49},{49,1},{2,18}... | collective-permute-start | bytes 1769480 | tf_op jit(solution)/shard_map/ppermute | solution.py:92
  256.8 47.6 %collective-permute-start.28 = (bf16[2,192,768]{2,1,0:T(8,128)(2,1)}, bf16[2,192,768]{2,1,0:T(8,128)(2,1)}, u32[]{:S(2)}, u32[]{:S(2)}) collective-permute-start(bf16[2,192,768]{2,1,0:T(8,128)(2,1)} %slice.1011), channel_id=1, source_target_pairs={{0,48},{16,0},{32,16},{48,32},{1,49},{17,1},{33,17},{49,33},{2,50}... | collective-permute-start | bytes 1769480 | tf_op jit(solution)/shard_map/ppermute | solution.py:92
  308.7 77.8 %collective-permute-start.31 = (bf16[2,1536,768]{2,1,0:T(8,128)(2,1)}, bf16[2,1536,768]{2,1,0:T(8,128)(2,1)}, u32[]{:S(2)}, u32[]{:S(2)}) collective-permute-start(bf16[2,1536,768]{2,1,0:T(8,128)(2,1)} %constant_dynamic-update-slice_fusion.5), channel_id=1, source_target_pairs={{0,4},{4,0},{1,5},{5,1},{2,6},{6,2},{3,7},{7,3},{8,12},{12,8},{9,1... | collective-permute-start | bytes 14155784 | tf_op jit(solution)/shard_map/ppermute | solution.py:92
  312.0 54.3 %collective-permute-start.30 = (bf16[2,384,1536]{2,1,0:T(8,128)(2,1)}, bf16[2,384,1536]{2,1,0:T(8,128)(2,1)S(1)}, u32[]{:S(2)}, u32[]{:S(2)}) collective-permute-start(bf16[2,384,1536]{2,1,0:T(8,128)(2,1)} %all-gather.2.cloned.1.call-done), channel_id=1, source_target_pairs={{0,72},{72,0},{8,64},{64,8},{1,73},{73,1},{9,65},{65,9},{2,74},{74... | collective-permute-start | bytes 7077896 | tf_op jit(solution)/shard_map/ppermute | solution.py:96
  325.9 47.7 %collective-permute-start.39 = (bf16[64,1536]{1,0:T(8,128)(2,1)S(1)}, bf16[64,1536]{1,0:T(8,128)(2,1)S(1)}, u32[]{:S(2)}, u32[]{:S(2)}) collective-permute-start(bf16[64,1536]{1,0:T(8,128)(2,1)S(1)} %slice.1044), channel_id=1, source_target_pairs={{0,1},{1,2},{2,3},{3,0},{4,5},{5,6},{6,7},{7,4},{8,9},{9,10},{10,1... | collective-permute-start | bytes 589832 | tf_op jit(solution)/shard_map/ppermute | solution.py:92
  397.6 196.9 %collective-permute-start.80 = (bf16[2,768,1536]{2,1,0:T(8,128)(2,1)}, bf16[2,768,1536]{2,1,0:T(8,128)(2,1)}, u32[]{:S(2)}, u32[]{:S(2)}) collective-permute-start(bf16[2,768,1536]{2,1,0:T(8,128)(2,1)} %pad_maximum_fusion.1), channel_id=1, source_target_pairs={{0,4},{4,0},{1,5},{5,1},{2,6},{6,2},{3,7},{7,3},{8,12},{12,8},{9,1... | collective-permute-start | bytes 14155784 | tf_op jit(solution)/shard_map/ppermute | solution.py:92
  436.6 225.7 %collective-permute-start.73 = (bf16[2,1536,768]{2,1,0:T(8,128)(2,1)}, bf16[2,1536,768]{2,1,0:T(8,128)(2,1)}, u32[]{:S(2)}, u32[]{:S(2)}) collective-permute-start(bf16[2,1536,768]{2,1,0:T(8,128)(2,1)} %pad_maximum_fusion), channel_id=1, source_target_pairs={{0,4},{4,0},{1,5},{5,1},{2,6},{6,2},{3,7},{7,3},{8,12},{12,8},{9,1... | collective-permute-start | bytes 14155784 | tf_op jit(solution)/shard_map/ppermute | solution.py:92
  566.7 178.6 %reduce-scatter.7.cloned.1.call-start = ((), (), s32[]{:S(2)}) async-start(), calls=%async_computation.10 | async-start | bytes 1474560
  593.8 173.8 %reduce-scatter.5.cloned.1.call-start = ((), (), s32[]{:S(2)}) async-start(), calls=%async_computation.9 | async-start | bytes 5898240 | tf_op jit(solution)/shard_map/reduce_scatter | solution.py:406
  714.8 37.5 %collective-permute-start.75 = (bf16[2,384,768]{2,1,0:T(8,128)(2,1)}, bf16[2,384,768]{2,1,0:T(8,128)(2,1)}, u32[]{:S(2)}, u32[]{:S(2)}) collective-permute-start(bf16[2,384,768]{2,1,0:T(8,128)(2,1)} %pad_maximum_fusion.6), channel_id=1, source_target_pairs={{0,16},{16,32},{32,48},{48,0},{1,17},{17,33},{33,49},{49,1},{2,18}... | collective-permute-start | bytes 3538952 | tf_op jit(solution)/shard_map/ppermute | solution.py:92
  720.3 41.8 %collective-permute-start.77 = (bf16[2,384,768]{2,1,0:T(8,128)(2,1)}, bf16[2,384,768]{2,1,0:T(8,128)(2,1)}, u32[]{:S(2)}, u32[]{:S(2)}) collective-permute-start(bf16[2,384,768]{2,1,0:T(8,128)(2,1)} %pad_maximum_fusion.7), channel_id=1, source_target_pairs={{0,48},{16,0},{32,16},{48,32},{1,49},{17,1},{33,17},{49,33},{2,50}... | collective-permute-start | bytes 3538952 | tf_op jit(solution)/shard_map/ppermute | solution.py:92
  (290 other events, 4140.2 us)
Sparse Core Ops, SparseCore 0:
  195.2 41.7 all-gather.1
  593.9 28.0 reduce-scatter.6
  624.4 60.5 reduce-scatter.4
